TPU v7x, 256 devices: a whole 4x4x8 slice. The times are simulated.
256 devices in a mesh: dp: 8 (over x_lo, y), tm: 32 (over x_hi, z, core).
Axes of the slice: x: 4 (x_hi: 2, x_lo: 2; x = x_hi * 2 + x_lo), y: 4, z: 8, core: 2. Of those that a mesh axis runs over, the one named last changes fastest.
Arguments:
- video_clips: bfloat16 [8, 128, 4, 24, 1024], P('dp', 'tm'), may hold values from -6 to 6
- kernel: bfloat16 [3, 3, 3, 1024, 1024], P(None, None, None, 'tm', 'dp'), may hold values from -0.0390625 to 0.0390625
- conv_bias: float32 [1024], P('dp'), may hold values from -3 to 3
- cotangent: bfloat16 [8, 64, 2, 12, 1024], P(None, 'tm', None, None, 'dp'), may hold values from -6 to 6
Outputs:
- sampled: bfloat16 [8, 64, 2, 12, 1024], P(None, 'tm', None, None, 'dp')
- clip_grad: bfloat16 [8, 128, 4, 24, 1024], P('dp', 'tm')
- kernel_grad: float32 [3, 3, 3, 1024, 1024], P(None, None, None, 'tm', 'dp')
- bias_grad: float32 [1024], P('dp')
All inputs are finite; a program needn't handle non-finite values.
Results may differ from a plain program's by a relative error of at most 0.019.
Values may be sent and summed in bfloat16 or wider, within the bound.
A program may use at most 192 MiB of HBM per device.

v0:
```python
import math

import jax
import jax.numpy as jnp
from jax import lax
from jax.sharding import PartitionSpec as P

tap_list = [(t_tap, h_tap, w_tap) for t_tap in range(3) for h_tap in range(3) for w_tap in range(3)]


def shifted(shard, axis, by):
    peers = lax.axis_size(axis)
    pairs = [(i, i + by) for i in range(peers) if 0 <= i + by < peers]
    return lax.ppermute(shard, axis, pairs)


def choose_line(values_in, tap_index, dim_index):
    length = values_in.shape[dim_index]
    even_part = lax.slice_in_dim(values_in, 0, length, 2, dim_index)
    odd_part = lax.slice_in_dim(values_in, 1, length, 2, dim_index)
    if tap_index == 1:
        return even_part
    if tap_index == 2:
        return odd_part
    leading = lax.slice_in_dim(odd_part, 0, odd_part.shape[dim_index] - 1, 1, dim_index)
    zero_line = jnp.zeros_like(lax.slice_in_dim(odd_part, 0, 1, 1, dim_index))
    return jnp.concatenate([zero_line, leading], axis=dim_index)


def tap_view(frames, rim_frame, t_tap, h_tap, w_tap):
    if t_tap == 1:
        picked = frames[:, 0::2]
    elif t_tap == 2:
        picked = frames[:, 1::2]
    else:
        picked = jnp.concatenate([rim_frame, frames[:, 1::2][:, :-1]], axis=1)
    return choose_line(choose_line(picked, h_tap, 2), w_tap, 3)


def conv_forward(frames, rim_frame, weights):
    channels = frames.shape[-1]
    result = None
    for t_tap, h_tap, w_tap in tap_list:
        tap_rows = tap_view(frames, rim_frame, t_tap, h_tap, w_tap)
        product = jnp.dot(
            tap_rows.reshape(-1, channels),
            weights[t_tap, h_tap, w_tap],
            preferred_element_type=jnp.float32,
        )
        result = product if result is None else result + product
    return result.reshape(tap_rows.shape[:-1] + (weights.shape[-1],))


def lift(values_in, dim_index):
    length = values_in.shape[dim_index]
    rest_part = lax.slice_in_dim(values_in, 1, length, 1, dim_index)
    zero_line = jnp.zeros_like(lax.slice_in_dim(values_in, 0, 1, 1, dim_index))
    return jnp.concatenate([rest_part, zero_line], axis=dim_index)


def spread_grad(grad_bf, weights):
    line_sets = {0: [(1, False)], 1: [(2, False), (0, True)]}
    frame_sets = {0: [(1, False)], 1: [(2, False), (0, True)], 2: [(0, False)]}
    classes = {}
    for frame_class in (0, 1, 2):
        source = grad_bf[:, :1] if frame_class == 2 else grad_bf
        for row_class in (0, 1):
            for col_class in (0, 1):
                moved_list = []
                matrices = []
                for t_tap, t_next in frame_sets[frame_class]:
                    for h_tap, h_next in line_sets[row_class]:
                        for w_tap, w_next in line_sets[col_class]:
                            moved = source
                            if t_next:
                                moved = lift(moved, 1)
                            if h_next:
                                moved = lift(moved, 2)
                            if w_next:
                                moved = lift(moved, 3)
                            moved_list.append(moved)
                            matrices.append(weights[t_tap, h_tap, w_tap])
                joined_rows = jnp.concatenate(moved_list, axis=4)
                joined_mats = jnp.concatenate(matrices, axis=1)
                classes[frame_class, row_class, col_class] = lax.dot_general(
                    joined_rows,
                    joined_mats,
                    (((4,), (1,)), ((), ())),
                    preferred_element_type=jnp.float32,
                )

    def weave(frame_class):
        row_pairs = [
            jnp.stack(
                [classes[frame_class, row_class, 0], classes[frame_class, row_class, 1]], axis=4
            )
            for row_class in (0, 1)
        ]
        return jnp.stack(row_pairs, axis=3)

    frame_pairs = jnp.stack([weave(0), weave(1)], axis=2)
    dims_out = frame_pairs.shape
    woven = frame_pairs.reshape(
        dims_out[0], dims_out[1] * 2, dims_out[3] * 2, dims_out[5] * 2, dims_out[7]
    )
    rim_part = weave(2)
    rim_dims = rim_part.shape
    rim_part = rim_part.reshape(rim_dims[0], 1, rim_dims[2] * 2, rim_dims[4] * 2, rim_dims[6])
    return jnp.concatenate([woven, rim_part], axis=1)


def kernel_terms(frames, rim_frame, grad_bf):
    channels = frames.shape[-1]
    right_rows = grad_bf.reshape(-1, grad_bf.shape[-1])
    stacked = []
    for t_tap, h_tap, w_tap in tap_list:
        tap_rows = tap_view(frames, rim_frame, t_tap, h_tap, w_tap)
        stacked.append(
            lax.dot_general(
                tap_rows.reshape(-1, channels),
                right_rows,
                (((0,), (0,)), ((), ())),
                preferred_element_type=jnp.float32,
            )
        )
    return jnp.stack(stacked).reshape((3, 3, 3, channels, right_rows.shape[-1]))


def shards(video_clips, kernel, conv_bias, cotangent):
    rim_frame = shifted(video_clips[:, -1:], "tm", 1)
    extended = jnp.concatenate([video_clips, rim_frame], axis=1)
    weights = lax.all_gather(kernel, "tm", axis=3, tiled=True)
    gathered = lax.all_gather(extended, "dp", axis=0, tiled=True)
    pre_act = conv_forward(gathered[:, :-1], gathered[:, -1:], weights)
    pre_act = pre_act + conv_bias
    sigmoid_val = jax.nn.sigmoid(pre_act)
    sampled = (pre_act * sigmoid_val).astype(jnp.bfloat16)
    slope_grad = cotangent.astype(jnp.float32) * sigmoid_val * (1.0 + pre_act * (1.0 - sigmoid_val))
    grad_bf = slope_grad.astype(jnp.bfloat16)
    positions = (
        grad_bf.shape[0]
        * grad_bf.shape[1]
        * lax.axis_size("tm")
        * grad_bf.shape[2]
        * grad_bf.shape[3]
    )
    inv_scale = 1.0 / math.sqrt(positions)
    bias_grad = lax.psum(jnp.sum(slope_grad, axis=(0, 1, 2, 3)) * inv_scale, "tm")
    summed = lax.psum_scatter(
        spread_grad(grad_bf, weights).astype(jnp.bfloat16), "dp", scatter_dimension=0, tiled=True
    ).astype(jnp.float32)
    carried = shifted(summed[:, -1:].astype(jnp.bfloat16), "tm", -1).astype(jnp.float32)
    last_index = video_clips.shape[1] - 1
    clip_grad = jnp.concatenate(
        [summed[:, :last_index], summed[:, last_index : last_index + 1] + carried], axis=1
    ).astype(jnp.bfloat16)
    kernel_term = kernel_terms(gathered[:, :-1], gathered[:, -1:], grad_bf)
    kernel_grad = lax.psum_scatter(
        (kernel_term * inv_scale).astype(jnp.bfloat16), "tm", scatter_dimension=3, tiled=True
    ).astype(jnp.float32)
    return (sampled, clip_grad, kernel_grad, bias_grad)


def solution(mesh):
    return jax.shard_map(
        shards,
        mesh=mesh,
        in_specs=(
            P("dp", "tm", None, None, None),
            P(None, None, None, "tm", "dp"),
            P("dp"),
            P(None, "tm", None, None, "dp"),
        ),
        out_specs=(
            P(None, "tm", None, None, "dp"),
            P("dp", "tm", None, None, None),
            P(None, None, None, "tm", "dp"),
            P("dp"),
        ),
        check_vma=False,
    )
```

profile of v0, /device:TPU:97, one launch (start us, length us, event | category | flops | bytes accessed | tf_op | source)
XLA Modules:
  0.0 734.8 jit_solution(1414445104247811877)
XLA Ops:
  19.1 93.0 %all-gather.5.cloned.1.call-done = bf16[3,3,3,1024,128]{4,3,2,1,0:T(8,128)(2,1)} async-done(((bf16[3,3,3,32,128]{4,3,2,1,0:T(8,128)(2,1)}), bf16[3,3,3,1024,128]{4,3,2,1,0:T(8,128)(2,1)}) %all-gather.5.cloned.1.call-update) | async-done | bytes 7077904 | tf_op jit(solution)/shard_map/all_gather | solution.py:132
  132.3 69.6 %all-gather.3.cloned.1.call-done = bf16[8,5,4,24,1024]{4,3,2,1,0:T(8,128)(2,1)} async-done(((bf16[1,5,4,24,1024]{4,3,2,1,0:T(8,128)(2,1)}), bf16[8,5,4,24,1024]{4,3,2,1,0:T(8,128)(2,1)}) %all-gather.3.cloned.1.call-update) | async-done | bytes 7864336 | tf_op jit(solution)/shard_map/all_gather | solution.py:133
  210.8 5.7 slice.202
  216.5 9.6 %slice.205 = bf16[8,2,2,12,1024]{4,3,2,1,0:T(8,128)(2,1)} slice(bf16[8,2,2,24,1024]{4,3,2,1,0:T(8,128)(2,1)} %copy-done.19), slice={[0:8:1], [0:2:1], [0:2:1], [0:24:2], [0:1024:1]} | slice | bytes 1572864 | tf_op jit(solution)/shard_map/slice | solution.py:19
  228.7 9.4 %slice.223 = bf16[8,2,2,12,1024]{4,3,2,1,0:T(8,128)(2,1)} slice(bf16[8,2,2,24,1024]{4,3,2,1,0:T(8,128)(2,1)} %concatenate.222), slice={[0:8:1], [0:2:1], [0:2:1], [1:24:2], [0:1024:1]} | slice | bytes 1572864 | tf_op jit(solution)/shard_map/slice | solution.py:20
  238.1 9.4 %slice.226 = bf16[8,2,2,12,1024]{4,3,2,1,0:T(8,128)(2,1)} slice(bf16[8,2,2,24,1024]{4,3,2,1,0:T(8,128)(2,1)} %concatenate.222), slice={[0:8:1], [0:2:1], [0:2:1], [0:24:2], [0:1024:1]} | slice | bytes 1572864 | tf_op jit(solution)/shard_map/slice | solution.py:19
  252.1 5.5 slice.180
  257.7 5.5 slice.183
  263.2 9.4 %slice.187 = bf16[8,2,2,12,1024]{4,3,2,1,0:T(8,128)(2,1)} slice(bf16[8,2,2,24,1024]{4,3,2,1,0:T(8,128)(2,1)} %get-tuple-element.48), slice={[0:8:1], [0:2:1], [0:2:1], [1:24:2], [0:1024:1]} | slice | bytes 1572864 | tf_op jit(solution)/shard_map/slice | solution.py:20
  272.6 9.5 %slice.190 = bf16[8,2,2,12,1024]{4,3,2,1,0:T(8,128)(2,1)} slice(bf16[8,2,2,24,1024]{4,3,2,1,0:T(8,128)(2,1)} %get-tuple-element.48), slice={[0:8:1], [0:2:1], [0:2:1], [0:24:2], [0:1024:1]} | slice | bytes 1572864 | tf_op jit(solution)/shard_map/slice | solution.py:19
  282.1 9.5 %slice.193 = bf16[8,2,2,12,1024]{4,3,2,1,0:T(8,128)(2,1)} slice(bf16[8,2,2,24,1024]{4,3,2,1,0:T(8,128)(2,1)} %copy-done.1), slice={[0:8:1], [0:2:1], [0:2:1], [1:24:2], [0:1024:1]} | slice | bytes 1572864 | tf_op jit(solution)/shard_map/slice | solution.py:20
  291.6 9.4 %slice.196 = bf16[8,2,2,12,1024]{4,3,2,1,0:T(8,128)(2,1)} slice(bf16[8,2,2,24,1024]{4,3,2,1,0:T(8,128)(2,1)} %copy-done.1), slice={[0:8:1], [0:2:1], [0:2:1], [0:24:2], [0:1024:1]} | slice | bytes 1572864 | tf_op jit(solution)/shard_map/slice | solution.py:19
  301.0 9.5 %slice.230 = bf16[8,2,2,12,1024]{4,3,2,1,0:T(8,128)(2,1)} slice(bf16[8,2,2,24,1024]{4,3,2,1,0:T(8,128)(2,1)} %get-tuple-element.44), slice={[0:8:1], [0:2:1], [0:2:1], [1:24:2], [0:1024:1]} | slice | bytes 1572864 | tf_op jit(solution)/shard_map/slice | solution.py:20
  310.5 9.4 %slice.233 = bf16[8,2,2,12,1024]{4,3,2,1,0:T(8,128)(2,1)} slice(bf16[8,2,2,24,1024]{4,3,2,1,0:T(8,128)(2,1)} %get-tuple-element.44), slice={[0:8:1], [0:2:1], [0:2:1], [0:24:2], [0:1024:1]} | slice | bytes 1572864 | tf_op jit(solution)/shard_map/slice | solution.py:19
  319.9 9.4 %slice.209 = bf16[8,2,2,12,1024]{4,3,2,1,0:T(8,128)(2,1)} slice(bf16[8,2,2,24,1024]{4,3,2,1,0:T(8,128)(2,1)} %get-tuple-element.66), slice={[0:8:1], [0:2:1], [0:2:1], [1:24:2], [0:1024:1]} | slice | bytes 1572864 | tf_op jit(solution)/shard_map/slice | solution.py:20
  329.3 9.4 %slice.212 = bf16[8,2,2,12,1024]{4,3,2,1,0:T(8,128)(2,1)} slice(bf16[8,2,2,24,1024]{4,3,2,1,0:T(8,128)(2,1)} %get-tuple-element.66), slice={[0:8:1], [0:2:1], [0:2:1], [0:24:2], [0:1024:1]} | slice | bytes 1572864 | tf_op jit(solution)/shard_map/slice | solution.py:19
  338.7 5.5 slice.236
  466.3 6.9 pad_maximum_fusion
  473.1 10.7 %copy.16 = bf16[8,2,2,2,2,12,2,1024]{7,0,6,5,4,3,2,1:T(8,128)(2,1)} copy(bf16[8,2,2,2,2,12,2,1024]{7,5,3,1,0,6,4,2:T(8,128)(2,1)} %pad_maximum_fusion) | data formatting | bytes 12582912 | tf_op jit(solution)/shard_map/stack | solution.py:101
  487.3 7.6 %copy.18 = bf16[8,5,4,24,1024]{4,3,2,1,0:T(8,128)(2,1)} copy(bf16[8,5,4,24,1024]{4,0,3,2,1:T(8,128)(2,1)S(1)} %pad_maximum_fusion.1) | data formatting | bytes 15728640 | tf_op jit(solution)/shard_map/concatenate | solution.py:109
  532.0 10.1 %multiply_convert_fusion = bf16[27,1024,128]{2,1,0:T(8,128)(2,1)} fusion(f32[27,1024,128]{2,1,0:T(8,128)} %fusion.19), kind=kLoop, calls=%fused_computation | loop fusion | flops 7077888 | bytes 21233664 | tf_op jit(solution)/shard_map/convert_element_type | solution.py:159
  543.7 40.5 %reduce-scatter.3.cloned.1.call-done = bf16[1,5,4,24,1024]{4,3,2,1,0:T(8,128)(2,1)} async-done(((bf16[8,5,4,24,1024]{4,3,2,1,0:T(8,128)(2,1)}), bf16[1,5,4,24,1024]{4,3,2,1,0:T(8,128)(2,1)}) %reduce-scatter.3.cloned.1.call-update) | async-done | bytes 983056 | tf_op jit(solution)/shard_map/reduce_scatter | solution.py:149
  587.7 49.7 %psum.7 = f32[128]{0:T(128)} all-reduce(f32[128]{0:T(128)S(1)} %broadcast_multiply_fusion), channel_id=1, replica_groups=mesh['dp'=8,'tm'=32] {'tm'}, use_global_device_ids=true, to_apply=%region_3.0 | all-reduce | flops 128 | bytes 1024 | tf_op jit(solution)/shard_map/psum | solution.py:148
  637.4 85.5 %reduce-scatter.5.cloned.1.call-done = bf16[3,3,3,32,128]{4,3,2,1,0:T(8,128)(2,1)} async-done(((bf16[3,3,3,1024,128]{4,3,2,1,0:T(8,128)(2,1)}), bf16[3,3,3,32,128]{4,3,2,1,0:T(8,128)(2,1)}) %reduce-scatter.5.cloned.1.call-update) | async-done | bytes 221200 | tf_op jit(solution)/shard_map/reduce_scatter | solution.py:158
  (329 shorter events, 219.4 us)
Async XLA Ops:
  7.2 104.9 %all-gather.5.cloned.1.call-start = ((), (), s32[]{:S(2)}) async-start(), calls=%async_computation.3 | async-start | bytes 7299072 | tf_op jit(solution)/shard_map/all_gather | solution.py:132
  7.9 194.0 %all-gather.3.cloned.1.call-start = ((), (), s32[]{:S(2)}) async-start(), calls=%async_computation.2 | async-start | bytes 8847360 | tf_op jit(solution)/shard_map/all_gather | solution.py:133
  8.9 7.9 %collective-permute-start = (bf16[1,1,4,24,1024]{4,3,2,1,0:T(8,128)(2,1)S(1)}, bf16[1,1,4,24,1024]{4,3,2,1,0:T(8,128)(2,1)S(1)}, u32[]{:S(2)}, u32[]{:S(2)}) collective-permute-start(bf16[1,1,4,24,1024]{4,3,2,1,0:T(8,128)(2,1)S(1)} %slice.173), channel_id=1, source_target_pairs={{0,1},{1,2},{2,3},{3,4},{4,5},{5,6},{6,7},{7,8},{8,9},{9,10},{10,1... | collective-permute-start | bytes 589832 | tf_op jit(solution)/shard_map/ppermute | solution.py:14
  19.0 565.2 %reduce-scatter.3.cloned.1.call-start = ((), (), s32[]{:S(2)}) async-start(), calls=%async_computation.4 | async-start | bytes 8847360 | tf_op jit(solution)/shard_map/reduce_scatter | solution.py:149
  216.5 31.1 %slice-start.3 = ((bf16[8,5,4,24,1024]{4,3,2,1,0:T(8,128)(2,1)}), bf16[8,1,4,24,1024]{4,3,2,1,0:T(8,128)(2,1)S(1)}, s32[]{:S(2)}) async-start(bf16[8,5,4,24,1024]{4,3,2,1,0:T(8,128)(2,1)} %all-gather.3.cloned.1.call-done), calls=%async_computation.9 | async-start | bytes 3145728 | tf_op jit(solution)/shard_map/slice | solution.py:134
  272.6 66.1 %copy-start = (bf16[8,2,2,24,1024]{4,3,2,1,0:T(8,128)(2,1)S(1)}, bf16[8,2,2,24,1024]{4,3,2,1,0:T(8,128)(2,1)}, u32[]{:S(2)}) copy-start(bf16[8,2,2,24,1024]{4,3,2,1,0:T(8,128)(2,1)} %get-tuple-element.45) | copy-start | bytes 4718596
  349.7 17.5 %copy-start.2 = (bf16[8,2,2,12,1024]{4,3,2,1,0:T(8,128)(2,1)S(1)}, bf16[8,2,2,12,1024]{4,3,2,1,0:T(8,128)(2,1)}, u32[]{:S(2)}) copy-start(bf16[8,2,2,12,1024]{4,3,2,1,0:T(8,128)(2,1)} %slice.223) | copy-start | bytes 2359300
  360.7 13.9 %copy-start.14 = (bf16[8,2,2,12,1024]{4,3,2,1,0:T(8,128)(2,1)S(1)}, bf16[8,2,2,12,1024]{4,3,2,1,0:T(8,128)(2,1)}, u32[]{:S(2)}) copy-start(bf16[8,2,2,12,1024]{4,3,2,1,0:T(8,128)(2,1)} %slice.187) | copy-start | bytes 2359300
  367.2 14.9 %copy-start.6 = (bf16[8,2,2,12,1024]{4,3,2,1,0:T(8,128)(2,1)S(1)}, bf16[8,2,2,12,1024]{4,3,2,1,0:T(8,128)(2,1)}, u32[]{:S(2)}) copy-start(bf16[8,2,2,12,1024]{4,3,2,1,0:T(8,128)(2,1)} %slice.230) | copy-start | bytes 2359300
  374.6 14.9 %copy-start.4 = (bf16[8,2,2,12,1024]{4,3,2,1,0:T(8,128)(2,1)S(1)}, bf16[8,2,2,12,1024]{4,3,2,1,0:T(8,128)(2,1)}, u32[]{:S(2)}) copy-start(bf16[8,2,2,12,1024]{4,3,2,1,0:T(8,128)(2,1)} %slice.236) | copy-start | bytes 2359300
  377.8 14.9 %copy-start.9 = (bf16[8,2,2,12,1024]{4,3,2,1,0:T(8,128)(2,1)S(1)}, bf16[8,2,2,12,1024]{4,3,2,1,0:T(8,128)(2,1)}, u32[]{:S(2)}) copy-start(bf16[8,2,2,12,1024]{4,3,2,1,0:T(8,128)(2,1)} %slice.215) | copy-start | bytes 2359300
  395.1 13.9 %copy-start.12 = (bf16[8,2,2,12,1024]{4,3,2,1,0:T(8,128)(2,1)S(1)}, bf16[8,2,2,12,1024]{4,3,2,1,0:T(8,128)(2,1)}, u32[]{:S(2)}) copy-start(bf16[8,2,2,12,1024]{4,3,2,1,0:T(8,128)(2,1)} %slice.193) | copy-start | bytes 2359300
  398.6 13.8 %copy-start.15 = (bf16[8,2,2,12,1024]{4,3,2,1,0:T(8,128)(2,1)S(1)}, bf16[8,2,2,12,1024]{4,3,2,1,0:T(8,128)(2,1)}, u32[]{:S(2)}) copy-start(bf16[8,2,2,12,1024]{4,3,2,1,0:T(8,128)(2,1)} %slice.187) | copy-start | bytes 2359300
  415.3 20.6 %slice-start = ((s8[7077888]{0:T(1024)(128)(4,1)}), s8[2883584]{0:T(1024)(128)(4,1)S(1)}, s32[]{:S(2)}) async-start(s8[7077888]{0:T(1024)(128)(4,1)} %bitcast.517), calls=%async_computation.6 | async-start | bytes 5767168
  425.2 10.7 %slice-start.1 = ((s8[7077888]{0:T(1024)(128)(4,1)}), s8[4194304]{0:T(1024)(128)(4,1)S(1)}, s32[]{:S(2)}) async-start(s8[7077888]{0:T(1024)(128)(4,1)} %bitcast.517), calls=%async_computation.7 | async-start | bytes 8388608
  425.2 10.7 %copy-start.48 = (bf16[384,1024]{1,0:T(8,128)(2,1)S(1)}, bf16[384,1024]{1,0:T(8,128)(2,1)}, u32[]{:S(2)}) copy-start(bf16[384,1024]{1,0:T(8,128)(2,1)} %reshape.187) | copy-start | bytes 2359300
  425.2 11.1 %copy-start.46 = (bf16[384,1024]{1,0:T(8,128)(2,1)S(1)}, bf16[384,1024]{1,0:T(8,128)(2,1)}, u32[]{:S(2)}) copy-start(bf16[384,1024]{1,0:T(8,128)(2,1)} %reshape.188) | copy-start | bytes 2359300
  425.3 11.5 %copy-start.44 = (bf16[384,1024]{1,0:T(8,128)(2,1)S(1)}, bf16[384,1024]{1,0:T(8,128)(2,1)}, u32[]{:S(2)}) copy-start(bf16[384,1024]{1,0:T(8,128)(2,1)} %reshape.189) | copy-start | bytes 2359300
  425.3 11.9 %copy-start.49 = (bf16[384,1024]{1,0:T(8,128)(2,1)S(1)}, bf16[384,1024]{1,0:T(8,128)(2,1)}, u32[]{:S(2)}) copy-start(bf16[384,1024]{1,0:T(8,128)(2,1)} %reshape.190) | copy-start | bytes 2359300
  425.3 12.3 %copy-start.40 = (bf16[384,1024]{1,0:T(8,128)(2,1)S(1)}, bf16[384,1024]{1,0:T(8,128)(2,1)}, u32[]{:S(2)}) copy-start(bf16[384,1024]{1,0:T(8,128)(2,1)} %reshape.191) | copy-start | bytes 2359300
  427.0 11.0 %copy-start.38 = (bf16[384,1024]{1,0:T(8,128)(2,1)S(1)}, bf16[384,1024]{1,0:T(8,128)(2,1)}, u32[]{:S(2)}) copy-start(bf16[384,1024]{1,0:T(8,128)(2,1)} %reshape.192) | copy-start | bytes 2359300
  429.3 9.1 %copy-start.47 = (bf16[384,1024]{1,0:T(8,128)(2,1)S(1)}, bf16[384,1024]{1,0:T(8,128)(2,1)}, u32[]{:S(2)}) copy-start(bf16[384,1024]{1,0:T(8,128)(2,1)} %reshape.193) | copy-start | bytes 2359300
  494.9 228.1 %reduce-scatter.5.cloned.1.call-start = ((), (), s32[]{:S(2)}) async-start(), calls=%async_computation.5 | async-start | bytes 7299072 | tf_op jit(solution)/shard_map/reduce_scatter | solution.py:158
  585.2 140.7 %collective-permute-start.1 = (bf16[1,1,4,24,1024]{4,3,2,1,0:T(8,128)(2,1)S(1)}, bf16[1,1,4,24,1024]{4,3,2,1,0:T(8,128)(2,1)S(1)}, u32[]{:S(2)}, u32[]{:S(2)}) collective-permute-start(bf16[1,1,4,24,1024]{4,3,2,1,0:T(8,128)(2,1)S(1)} %slice.307), channel_id=1, source_target_pairs={{1,0},{2,1},{3,2},{4,3},{5,4},{6,5},{7,6},{8,7},{9,8},{10,9},{11,1... | collective-permute-start | bytes 589832 | tf_op jit(solution)/shard_map/ppermute | solution.py:14
  (56 other events, 168.8 us)
Sparse Core Ops, SparseCore 0:
  10.6 101.4 all-gather.4
  113.8 88.0 all-gather.2
  495.0 89.1 reduce-scatter.2
  588.4 134.5 reduce-scatter.4
where the time goes:
time: 749 us; the launch traced here: 735 us
  waiting for transfers between devices  292 us (39%)
  local copies, waits for them, and re-layouts  268 us (36%)
  matrix products  68 us (9%)
  blocking collectives  49.7 us (7%)
  other arithmetic  33.7 us (4%)
  between operations  15.5 us (2%)
  starting transfers between devices  8.01 us (1%)
    all_gather x1, waiting for transfers between devices, shards(): weights = lax.all_gather(kernel, 'tm', axis=3, tiled=True)  93 us
    reduce_scatter x1, waiting for transfers between devices, shards(): lax.psum_scatter((kernel_term * inv_scale).astype(jnp.bfloat16), 'tm', sc...  85.5 us
    slice x11, local copies, waits for them, and re-layouts, choose_line(): even_part = lax.slice_in_dim(values_in, 0, length, 2, dim_index)  77.2 us
    all_gather x1, waiting for transfers between devices, shards(): gathered = lax.all_gather(extended, 'dp', axis=0, tiled=True)  69.6 us
    slice x9, local copies, waits for them, and re-layouts, choose_line(): odd_part = lax.slice_in_dim(values_in, 1, length, 2, dim_index)  69.4 us
    reshape x27, local copies, waits for them, and re-layouts, conv_forward(): tap_rows.reshape(-1, channels)  50.4 us
    psum x1, blocking collectives, shards(): lax.psum(jnp.sum(slope_grad, axis=(0, 1, 2, 3)) * inv_scale, 'tm')  49.7 us
    reduce_scatter x1, waiting for transfers between devices, shards(): lax.psum_scatter(spread_grad(grad_bf, weights).astype(jnp.bfloat16), 'dp'...  40.5 us
  transfers between devices with their start and end apart: 6, of which 5 were waited for; matrix products, arithmetic and copies ran while one was open for 10% of the time, Pallas kernels for 0%

commit v1 on v0

v1 whole, which is shorter than its diff:
```python
import math

import jax
import jax.numpy as jnp
import numpy as np
from jax import lax
from jax.experimental import pallas as pl
from jax.experimental.pallas import tpu as pltpu
from jax.sharding import PartitionSpec as P

MESH = pl.DeviceIdType.MESH
F32 = jnp.float32
BF16 = jnp.bfloat16
POSITIONS = 12288


def tap_gather():
    table = np.zeros((224, 96), np.float32)
    for h in range(3):
        for w in range(3):
            for r in range(2):
                for q in range(12):
                    row, col = 2 * r + h - 1, 2 * q + w - 1
                    if 0 <= row < 4 and 0 <= col < 24:
                        table[(h * 3 + w) * 24 + r * 12 + q, row * 24 + col] = 1.0
    return table


def kernel(
    x_ref, w_ref, cot_ref, bias_ref, gat_ref, sca_ref,
    samp_out, dx_out, dw_out, db_out,
    land, halo, wg, cotl, biasl, im_e, im_o, pacc, part, rsl, sbuf, sland, gbuf, ghalo, bz, bs, bl,
    d_e, d_o, dxb, dxp, dxs, dxl, dwb, dws, dwr, dwl, kout, dbo,
    x_send, x_recv, f_send, h_sem, w_send, w_recv, c_send, c_recv, b_send, b_recv, rs_send, rs_recv,
    s_send, s_recv, ag_send, ag_recv, bz_send, bz_recv, gh_sem, bs_send, bs_recv, dxp_send, dxp_recv,
    dx_send, dx_recv, k1_send, k1_recv, k2_send, k2_recv, o_sem,
):
    dp, tm = lax.axis_index("dp"), lax.axis_index("tm")
    xl, y = lax.div(dp, 4), lax.rem(dp, 4)
    xh, z, c = lax.div(tm, 16), lax.rem(lax.div(tm, 2), 8), lax.rem(tm, 2)
    primary = c == xl
    inv = 1.0 / math.sqrt(POSITIONS)

    def dev(xl_, y_, xh_, z_, c_):
        return (xl_ * 4 + y_, (xh_ * 8 + z_) * 2 + c_)

    def remote(src, dst, send, recv, device):
        return pltpu.make_async_remote_copy(
            src_ref=src, dst_ref=dst, send_sem=send, recv_sem=recv, device_id=device, device_id_type=MESH
        )

    def landed(dst, sem):
        pltpu.make_async_copy(dst, dst, sem).wait()

    def plus(a, by, n):
        return lax.rem(a + by, n)

    partner = dev(1 - xl, y, xh, z, c)
    sibling = dev(xl, y, xh, z, 1 - c)
    across = dev(xl, y, 1 - xh, z, c)

    barrier = pltpu.get_barrier_semaphore()
    peers = [partner]
    for dz in range(8):
        for dc in range(2):
            if dz or dc:
                peers.append(dev(xl, y, xh, plus(z, dz, 8), plus(c, dc, 2)))
    for dy in range(4):
        for dh in range(2):
            for dc in range(2):
                if dy or dh:
                    peers.append(dev(xl, plus(y, dy, 4), plus(xh, dh, 2), z, plus(c, dc, 2)))
    for peer in peers:
        pl.semaphore_signal(barrier, inc=1, device_id=peer, device_id_type=MESH)
    pl.semaphore_wait(barrier, len(peers))

    ends = []

    me_k = 2 * z + c
    for n, dz in enumerate((1, 7, 2, 6, 3, 5, 4)):
        zt = plus(z, dz, 8)
        copy = remote(x_ref.at[zt], land.at[me_k], x_send.at[n], x_recv.at[me_k], dev(xl, y, xh, zt, xl))
        copy.start()
        ends.append(copy.wait_send)
    own_x = pltpu.make_async_copy(x_ref.at[z], land.at[me_k], x_recv.at[me_k])
    sib_x = remote(x_ref.at[z], land.at[me_k], x_send.at[7], x_recv.at[me_k], dev(xl, y, xh, z, 1 - c))

    @pl.when(primary)
    def _():
        own_x.start()

    @pl.when(jnp.logical_not(primary))
    def _():
        sib_x.start()

    def w_at(h_, c_, y_):
        return wg.at[:, pl.ds(pl.multiple_of((h_ * 2 + c_) * 32, 32), 32), pl.ds(pl.multiple_of(y_ * 128, 128), 128)]

    def w_sem(h_, c_, y_):
        return w_recv.at[(h_ * 2 + c_) * 4 + y_]

    w_count = [0]

    def w_push(src, h_, c_, y_, device):
        copy = remote(src, w_at(h_, c_, y_), w_send.at[w_count[0]], w_sem(h_, c_, y_), device)
        w_count[0] += 1
        copy.start()
        ends.append(copy.wait_send)

    w_push(w_ref, xh, c, y, across)
    for dy in (1, 3, 2):
        w_push(w_ref, xh, c, y, dev(xl, plus(y, dy, 4), xh, z, c))
    w_push(w_ref, xh, c, y, sibling)
    pltpu.make_async_copy(w_ref, w_at(xh, c, y), w_sem(xh, c, y)).start()

    for dy in range(4):
        for dc in range(2):
            yd, cd = plus(y, dy, 4), plus(c, dc, 2)
            src, dst, sem = cot_ref.at[cd * 4 + yd], cotl.at[c, y], c_recv.at[c * 4 + y]
            if dy or dc:
                copy = remote(src, dst, c_send.at[dy * 2 + dc], sem, dev(xl, yd, xh, z, cd))
                copy.start()
                ends.append(copy.wait_send)
            else:
                pltpu.make_async_copy(src, dst, sem).start()
    pltpu.make_async_copy(bias_ref, biasl.at[y], b_recv.at[y]).start()
    for dy in range(1, 4):
        copy = remote(bias_ref, biasl.at[y], b_send.at[dy], b_recv.at[y], dev(xl, plus(y, dy, 4), xh, z, c))
        copy.start()
        ends.append(copy.wait_send)

    def spread(j, carry):
        dz = jnp.where(lax.rem(j, 2) == 1, lax.div(j + 1, 2), lax.rem(8 - lax.div(j, 2), 8))
        zs = plus(z, dz, 8)
        for cs in range(2):
            k = 2 * zs + cs
            landed(land.at[k], x_recv.at[k])

            @pl.when(primary)
            def _():
                remote(land.at[k], land.at[k], f_send.at[k], x_recv.at[k], partner).start()

        for cs in range(2):
            k = 2 * zs + cs
            frames = land[k]
            side = jnp.concatenate([frames[i * 96:(i + 1) * 96] for i in range(4)], axis=1)
            taps = jnp.dot(gat_ref[...], side, preferred_element_type=F32)
            for i in range(4):
                piece = taps[:216, i * 128:(i + 1) * 128].reshape(9, 24, 128)
                if i % 2 == 0:
                    im_e[:, 2 * k + i // 2] = piece
                else:
                    im_o[:, 2 * k + 1 + i // 2] = piece
        return carry

    lax.fori_loop(0, 2, spread, 0)
    landed(w_at(1 - xh, c, y), w_sem(1 - xh, c, y))
    for dy in (1, 3, 2):
        w_push(w_at(1 - xh, c, y), 1 - xh, c, y, dev(xl, plus(y, dy, 4), xh, z, c))
    w_push(w_at(1 - xh, c, y), 1 - xh, c, y, sibling)
    lax.fori_loop(2, 8, spread, 0)

    halo_copy = remote(land.at[15, pl.ds(288, 96)], halo, h_sem.at[0], h_sem.at[1], across)
    halo_copy.start()
    ends.append(halo_copy.wait_send)
    for dy in (1, 3, 2):
        for h_ in (xh, 1 - xh):
            yd = plus(y, dy, 4)
            landed(w_at(h_, c, yd), w_sem(h_, c, yd))
            w_push(w_at(h_, c, yd), h_, c, yd, sibling)
    landed(w_at(xh, c, y), w_sem(xh, c, y))
    for dy in range(4):
        for h_ in (xh, 1 - xh):
            yd = plus(y, dy, 4)
            landed(w_at(h_, 1 - c, yd), w_sem(h_, 1 - c, yd))

    def forward(half):
        base = 16 * half

        def step(h, carry):
            lhs, rhs = [], []
            for w in range(3):
                hw = h * 3 + w
                lhs.append(im_o[hw, pl.ds(base, 16)].reshape(384, 128).astype(BF16))
                lhs.append(im_e[hw, pl.ds(base, 16)].reshape(384, 128).astype(BF16))
                lhs.append(im_o[hw, pl.ds(base + 1, 16)].reshape(384, 128).astype(BF16))
                rhs += [wg[hw], wg[9 + hw], wg[18 + hw]]
            pacc[...] += jnp.dot(
                jnp.concatenate(lhs, axis=1), jnp.concatenate(rhs, axis=0), preferred_element_type=F32
            )
            return carry

        pacc[...] = jnp.zeros_like(pacc)
        lax.fori_loop(0, 3, step, 0)
        for q in range(4):
            zt = 4 * half + q
            part[zt] = pacc[q * 96:(q + 1) * 96].astype(BF16)
            copy = remote(part.at[zt], rsl.at[z], rs_send.at[zt], rs_recv.at[z], dev(xl, y, xh, zt, c))

            @pl.when(z != zt)
            def _(copy=copy):
                copy.start()

    forward(1)
    landed(halo, h_sem.at[1])
    rim = jnp.dot(gat_ref[...], halo[...], preferred_element_type=F32)[:216].reshape(9, 24, 128)
    im_o[:, 0] = jnp.where(xh == 1, rim, jnp.zeros_like(rim))
    forward(0)

    for dy in range(4):
        yd = plus(y, dy, 4)
        landed(biasl.at[yd], b_recv.at[yd])
        for cs in range(2):
            landed(cotl.at[cs, yd], c_recv.at[cs * 4 + yd])
    pre = part[z].astype(F32)
    for dz in (1, 7, 2, 6, 3, 5, 4):
        zs = plus(z, dz, 8)
        landed(rsl.at[zs], rs_recv.at[zs])
        pre = pre + rsl[zs].astype(F32)
    pre = pre + jnp.concatenate([biasl[i, 0:1] for i in range(4)], axis=1)
    sig = 1.0 / (1.0 + jnp.exp(-pre))
    samp = (pre * sig).astype(BF16)
    cot = jnp.concatenate(
        [jnp.concatenate([cotl[cs, i] for i in range(4)], axis=1) for cs in range(2)], axis=0
    ).astype(F32)
    slope = cot * sig * (1.0 + pre * (1.0 - sig))
    gbuf[z] = slope.astype(BF16)
    bz[z] = jnp.broadcast_to(jnp.sum(slope, axis=0, keepdims=True), (8, 512))
    for n, dz in enumerate((1, 7, 2, 6, 3, 5, 4)):
        zt = plus(z, dz, 8)
        copy = remote(gbuf.at[z], gbuf.at[z], ag_send.at[n], ag_recv.at[z], dev(xl, y, xh, zt, c))
        copy.start()
        ends.append(copy.wait_send)
        copy = remote(bz.at[z], bz.at[z], bz_send.at[n], bz_recv.at[z], dev(xl, y, xh, zt, c))
        copy.start()
        ends.append(copy.wait_send)
    for cs in range(2):
        for i in range(4):
            sbuf[cs, i] = samp[cs * 48:(cs + 1) * 48, i * 128:(i + 1) * 128]
    for dy in range(4):
        for dc in range(2):
            yd, cd = plus(y, dy, 4), plus(c, dc, 2)
            src, dst, sem = sbuf.at[cd, yd], sland.at[c * 4 + y], s_recv.at[c * 4 + y]
            if dy or dc:
                copy = remote(src, dst, s_send.at[dy * 2 + dc], sem, dev(xl, yd, xh, z, cd))
                copy.start()
                ends.append(copy.wait_send)
            else:
                pltpu.make_async_copy(src, dst, sem).start()
    for dz in (1, 7, 2, 6, 3, 5, 4):
        zs = plus(z, dz, 8)
        landed(gbuf.at[zs], ag_recv.at[zs])
    ghalo_copy = remote(gbuf.at[0, pl.ds(0, 32)], ghalo, gh_sem.at[0], gh_sem.at[1], across)
    ghalo_copy.start()
    ends.append(ghalo_copy.wait_send)

    def back(hw, carry):
        mats = jnp.concatenate([wg[hw], wg[9 + hw], wg[18 + hw]], axis=0)
        r = lax.dot_general(
            gbuf[...].reshape(768, 512), mats, (((1,), (1,)), ((), ())), preferred_element_type=F32
        )
        d_e[hw] = r[:, 128:256].reshape(32, 24, 128)
        d_o[hw, pl.ds(0, 31)] = (r[:744, 256:] + r[24:, :128]).reshape(31, 24, 128)
        d_o[hw, 31] = r[744:, 256:]
        return carry

    lax.fori_loop(0, 9, back, 0)
    landed(ghalo, gh_sem.at[1])

    def back_rim(hw, carry):
        r = lax.dot_general(ghalo[...], wg[hw], (((1,), (1,)), ((), ())), preferred_element_type=F32)
        d_o[hw, 31] += jnp.where(xh == 0, r[:24], jnp.zeros_like(r[:24]))
        return carry

    lax.fori_loop(0, 9, back_rim, 0)

    def gather_back(k, carry):
        cols = []
        for i in range(4):
            held = d_e if i % 2 == 0 else d_o
            cols.append(held[:, 2 * k + i // 2].reshape(216, 128))
        side = jnp.concatenate(cols, axis=1)
        side = jnp.concatenate([side, jnp.zeros((8, 512), F32)], axis=0).astype(BF16)
        r = jnp.dot(sca_ref[...], side, preferred_element_type=F32).astype(BF16)
        for i in range(4):
            dxb[k, pl.ds(i * 96, 96)] = r[:, i * 128:(i + 1) * 128]

        @pl.when(jnp.logical_not(primary))
        def _():
            remote(dxb.at[k], dxp.at[k], dxp_send.at[k], dxp_recv.at[k], partner).start()

        return carry

    lax.fori_loop(0, 16, gather_back, 0)

    def send_back(k, carry):
        landed(dxp.at[k], dxp_recv.at[k])
        dxs[k] = (dxb[k].astype(F32) + dxp[k].astype(F32)).astype(BF16)

        @pl.when(k == me_k)
        def _():
            pltpu.make_async_copy(dxs.at[k], dxl.at[z], dx_recv.at[z]).start()

        @pl.when(k != me_k)
        def _():
            remote(
                dxs.at[k], dxl.at[z], dx_send.at[k], dx_recv.at[z], dev(xl, y, xh, lax.div(k, 2), lax.rem(k, 2))
            ).start()

        return carry

    def some_back(first, last):
        @pl.when(primary)
        def _():
            lax.fori_loop(first, last, send_back, 0)

    for h in range(3):
        def grad_step(w, carry, h=h):
            hw = h * 3 + w
            lhs = jnp.concatenate(
                [
                    im_o[hw, pl.ds(0, 32)].reshape(768, 128).astype(BF16),
                    im_e[hw].reshape(768, 128).astype(BF16),
                    im_o[hw, pl.ds(1, 32)].reshape(768, 128).astype(BF16),
                ],
                axis=1,
            )
            r = lax.dot_general(
                lhs, gbuf[...].reshape(768, 512), (((0,), (0,)), ((), ())), preferred_element_type=F32
            ).astype(BF16)
            for t in range(3):
                for h_ in range(2):
                    for c_ in range(2):
                        at = t * 128 + h_ * 64 + c_ * 32
                        dwb[h, c_, h_, w * 3 + t] = r[at:at + 32]
            return carry

        lax.fori_loop(0, 3, grad_step, 0)
        copy = remote(dwb.at[h, 1 - c], dws.at[h], k1_send.at[h], k1_recv.at[h], sibling)
        copy.start()
        ends.append(copy.wait_send)
        some_back(4 * h, 4 * h + 4)

    for h in range(3):
        landed(dws.at[h], k1_recv.at[h])

        def add_step(n, carry, h=h):
            for h_ in range(2):
                dwr[h, h_, n] = (dwb[h, c, h_, n].astype(F32) + dws[h, h_, n].astype(F32)).astype(BF16)
            return carry

        lax.fori_loop(0, 9, add_step, 0)
        slot = xh * 4 + y
        for dh in range(2):
            for dy in range(4):
                yd, hd = plus(y, dy, 4), plus(xh, dh, 2)
                src = dwr.at[h, hd, :, :, pl.ds(pl.multiple_of(yd * 128, 128), 128)]
                dst, sem = dwl.at[h, slot], k2_recv.at[h * 8 + slot]
                if dh or dy:
                    copy = remote(src, dst, k2_send.at[h * 8 + dh * 4 + dy], sem, dev(xl, yd, hd, z, c))
                    copy.start()
                    ends.append(copy.wait_send)
                else:
                    pltpu.make_async_copy(src, dst, sem).start()
    some_back(12, 16)

    total = bz[z, 0:1]
    for dz in (1, 7, 2, 6, 3, 5, 4):
        zs = plus(z, dz, 8)
        landed(bz.at[zs], bz_recv.at[zs])
        total = total + bz[zs, 0:1]
    for i in range(4):
        bs[i] = jnp.broadcast_to(total[:, i * 128:(i + 1) * 128], (8, 128))
    slot_b = (xh * 2 + c) * 4 + y
    for dy in range(4):
        for dh in range(2):
            for dc in range(2):
                yd, hd, cd = plus(y, dy, 4), plus(xh, dh, 2), plus(c, dc, 2)
                if dy or dh or dc:
                    copy = remote(
                        bs.at[yd], bl.at[slot_b], bs_send.at[(dy * 2 + dh) * 2 + dc], bs_recv.at[slot_b],
                        dev(xl, yd, hd, z, cd),
                    )
                    copy.start()
                    ends.append(copy.wait_send)
                else:
                    pltpu.make_async_copy(bs.at[y], bl.at[slot_b], bs_recv.at[slot_b]).start()

    outs = []
    for i in range(8):
        landed(sland.at[i], s_recv.at[i])
    outs.append(pltpu.make_async_copy(sland, samp_out, o_sem.at[0]))
    outs[-1].start()

    for h in range(3):
        for i in range(8):
            landed(dwl.at[h, i], k2_recv.at[h * 8 + i])

        def sum_step(w, carry, h=h):
            for t in range(3):
                acc = dwl[h, 0, w * 3 + t].astype(F32)
                for i in range(1, 8):
                    acc = acc + dwl[h, i, w * 3 + t].astype(F32)
                kout[t * 9 + h * 3 + w] = acc * inv
            return carry

        lax.fori_loop(0, 3, sum_step, 0)
    outs.append(pltpu.make_async_copy(kout, dw_out, o_sem.at[1]))
    outs[-1].start()

    acc = None
    for i in range(16):
        landed(bl.at[i], bs_recv.at[i])
        acc = bl[i] if acc is None else acc + bl[i]
    dbo[...] = acc * inv
    outs.append(pltpu.make_async_copy(dbo, db_out, o_sem.at[2]))
    outs[-1].start()

    for i in range(8):
        landed(dxl.at[i], dx_recv.at[i])
    outs.append(pltpu.make_async_copy(dxl, dx_out, o_sem.at[3]))
    outs[-1].start()

    for end in ends:
        end()

    @pl.when(jnp.logical_not(primary))
    def _():
        sib_x.wait_send()

        def drain(k, carry):
            remote(dxb.at[k], dxp.at[k], dxp_send.at[k], dxp_recv.at[k], partner).wait_send()
            return carry

        lax.fori_loop(0, 16, drain, 0)

    @pl.when(primary)
    def _():
        def drain(k, carry):
            remote(land.at[k], land.at[k], f_send.at[k], x_recv.at[k], partner).wait_send()

            @pl.when(k != me_k)
            def _():
                remote(
                    dxs.at[k], dxl.at[z], dx_send.at[k], dx_recv.at[z],
                    dev(xl, y, xh, lax.div(k, 2), lax.rem(k, 2)),
                ).wait_send()

            return carry

        lax.fori_loop(0, 16, drain, 0)

    for zt in range(8):
        copy = remote(part.at[zt], rsl.at[z], rs_send.at[zt], rs_recv.at[z], dev(xl, y, xh, zt, c))

        @pl.when(z != zt)
        def _(copy=copy):
            copy.wait_send()

    for out in outs:
        out.wait()


def shards(video_clips, weights, conv_bias, cotangent):
    x = video_clips.reshape(384, 2, 8, 64).transpose(2, 0, 1, 3).reshape(8, 384, 128)
    w = weights.reshape(27, 32, 128)
    cot = cotangent.reshape(8, 48, 128)
    bias = jnp.broadcast_to(conv_bias.reshape(1, 128), (8, 128))
    table = tap_gather()
    gat = jnp.asarray(table, BF16)
    sca = jnp.asarray(table.T, BF16)
    any_spec = pl.BlockSpec(memory_space=pl.ANY)
    vmem_spec = pl.BlockSpec(memory_space=pltpu.VMEM)

    def v(shape, dtype=BF16):
        return pltpu.VMEM(shape, dtype)

    def sems(n):
        return pltpu.SemaphoreType.DMA((n,))

    samp, dx, dw, db = pl.pallas_call(
        kernel,
        out_shape=[
            jax.ShapeDtypeStruct((8, 48, 128), BF16),
            jax.ShapeDtypeStruct((8, 384, 128), BF16),
            jax.ShapeDtypeStruct((27, 32, 128), F32),
            jax.ShapeDtypeStruct((8, 128), F32),
        ],
        in_specs=[any_spec] * 4 + [vmem_spec] * 2,
        out_specs=[any_spec] * 4,
        scratch_shapes=[
            v((16, 384, 128)),
            v((96, 128)),
            v((27, 128, 512)),
            v((2, 4, 48, 128)),
            v((4, 8, 128), F32),
            v((9, 32, 24, 128), F32),
            v((9, 33, 24, 128), F32),
            v((384, 512), F32),
            v((8, 96, 512)),
            v((8, 96, 512)),
            v((2, 4, 48, 128)),
            v((8, 48, 128)),
            v((8, 96, 512)),
            v((32, 512)),
            v((8, 8, 512), F32),
            v((4, 8, 128), F32),
            v((16, 8, 128), F32),
            v((9, 32, 24, 128), F32),
            v((9, 32, 24, 128), F32),
            v((16, 384, 128)),
            v((16, 384, 128)),
            v((16, 384, 128)),
            v((8, 384, 128)),
            v((3, 2, 2, 9, 32, 512)),
            v((3, 2, 9, 32, 512)),
            v((3, 2, 9, 32, 512)),
            v((3, 8, 9, 32, 128)),
            v((27, 32, 128), F32),
            v((8, 128), F32),
            sems(8), sems(16), sems(16), sems(2),
            sems(16), sems(16), sems(8), sems(8), sems(4), sems(4),
            sems(8), sems(8), sems(8), sems(8), sems(8), sems(8), sems(8), sems(8),
            sems(2), sems(16), sems(16), sems(16), sems(16), sems(16), sems(8),
            sems(3), sems(3), sems(24), sems(24), sems(4),
        ],
        compiler_params=pltpu.CompilerParams(
            collective_id=0, has_side_effects=True, vmem_limit_bytes=60 * 1024 * 1024
        ),
        cost_estimate=pl.CostEstimate(flops=10_000_000_000, bytes_accessed=8_000_000, transcendentals=50_000),
    )(x, w, cot, bias, gat, sca)
    sampled = samp.reshape(8, 2, 2, 12, 128)
    clip_grad = dx.reshape(8, 384, 2, 64).transpose(1, 2, 0, 3).reshape(1, 4, 4, 24, 1024)
    return sampled, clip_grad, dw.reshape(3, 3, 3, 32, 128), db[0]


def solution(mesh):
    return jax.shard_map(
        shards,
        mesh=mesh,
        in_specs=(
            P("dp", "tm", None, None, None),
            P(None, None, None, "tm", "dp"),
            P("dp"),
            P(None, "tm", None, None, "dp"),
        ),
        out_specs=(
            P(None, "tm", None, None, "dp"),
            P("dp", "tm", None, None, None),
            P(None, None, None, "tm", "dp"),
            P("dp"),
        ),
        check_vma=False,
    )
```

time: 749 us -> 150 us (0.20)
  the two profiles are of different devices: /device:TPU:97 before, /device:TPU:7 now
where the time goes in v1:
time: 150 us
  Pallas kernels  133 us (89%)
  local copies, waits for them, and re-layouts  15.9 us (11%)
    pallas_call x1, Pallas kernels, shards(): pl.pallas_call(kernel, out_shape=[jax.ShapeDtypeStruct((8, 48, 128), BF16...  133 us
    reshape x2, local copies, waits for them, and re-layouts, shards(): video_clips.reshape(384, 2, 8, 64).transpose(2, 0, 1, 3)  3.65 us

profile of v1, /device:TPU:7, one launch (start us, length us, event | category | flops | bytes accessed | tf_op | source)
XLA Modules:
  0.0 149.7 jit_solution(17653136402943287332)
XLA Ops:
  0.6 1.2 broadcast_in_dim.2.bias_ref
  1.9 0.9 copy.15
  2.8 0.7 copy.17.cot_ref
  3.5 2.5 %reshape.34 = bf16[384,2,8,64]{3,2,1,0:T(8,128)(2,1)S(1)} reshape(bf16[1,4,4,24,1024]{4,3,2,1,0:T(8,128)(2,1)} %param.6) | data formatting | bytes 1572864 | tf_op jit(solution)/shard_map/reshape | solution.py:465
  6.0 1.2 copy.14
  7.1 1.2 copy.16.x_ref
  8.3 133.1 %shard_map.93 = (bf16[8,48,128]{2,1,0:T(8,128)(2,1)}, bf16[8,384,128]{2,1,0:T(8,128)(2,1)}, f32[27,32,128]{2,1,0:T(8,128)}, f32[8,128]{1,0:T(8,128)}) custom-call(bf16[8,384,128]{2,1,0:T(8,128)(2,1)} %copy.16.x_ref, bf16[27,32,128]{2,1,0:T(8,128)(2,1)} %bitcast.21, bf16[8,48,128]{2,1,0:T(8,128)(2,1)} %copy.17.cot_ref, f32[8,128]{1,0:T(8,128)} %broadcast_in_dim.2.bias_ref, ...), custom_call_target="tpu_custom_call" | custom-call | flops 10000000000 | bytes 8000000 | tf_op jit(solution)/shard_map/pallas_call | solution.py:481
  141.4 0.9 copy.18
  142.3 0.7 copy.21
  143.1 1.2 slice_bitcast_fusion
  144.3 1.5 copy.19
  145.7 1.3 copy.20
  147.0 0.0 copy-start
  147.1 1.9 %reshape.40 = bf16[1,4,4,24,1024]{4,3,2,1,0:T(8,128)(2,1)} reshape(bf16[384,2,8,64]{3,2,1,0:T(8,128)(2,1)S(1)} %copy.20) | data formatting | bytes 1572864 | tf_op jit(solution)/shard_map/reshape | solution.py:533
  148.9 0.0 copy-done
  148.9 0.8 copy.23
Async XLA Ops:
  147.0 1.9 %copy-start = (f32[27,32,128]{2,1,0:T(8,128)S(1)}, f32[27,32,128]{2,1,0:T(8,128)}, u32[]{:S(2)}) copy-start(f32[27,32,128]{2,1,0:T(8,128)} %get-tuple-element.10) | copy-start | bytes 1327108

commit v2 on v1

v2 whole, which is shorter than its diff:
```python
import math

import jax
import jax.numpy as jnp
import numpy as np
from jax import lax
from jax.experimental import pallas as pl
from jax.experimental.pallas import tpu as pltpu
from jax.sharding import PartitionSpec as P

MESH = pl.DeviceIdType.MESH
F32 = jnp.float32
BF16 = jnp.bfloat16
POSITIONS = 12288


def tap_gather():
    table = np.zeros((224, 96), np.float32)
    for h in range(3):
        for w in range(3):
            for r in range(2):
                for q in range(12):
                    row, col = 2 * r + h - 1, 2 * q + w - 1
                    if 0 <= row < 4 and 0 <= col < 24:
                        table[(h * 3 + w) * 24 + q * 2 + r, row * 24 + col] = 1.0
    return table


def kernel(
    x_ref, w_ref, cot_ref, bias_ref, gat_ref, sca_ref,
    samp_out, dx_out, dw_out, db_out,
    xv, xp, land, halo, wg, cotl, biasb, biasl, im_e, im_o, pacc, part, rsl, sbuf, sland, gbuf, bz, bs, bl,
    dtmp, dxb, dxp, dxs, dxl, dxo, dwb, dws, dwr, dwl, dwo, dwx, dwy, kout, dbo,
    v_sem, x_send, x_recv, f_send, h_sem, w_send, w_recv, c_send, c_recv, b_send, b_recv, rs_send, rs_recv,
    s_send, s_recv, ag_send, ag_recv, bz_send, bz_recv, gh_send, gh_recv, bs_send, bs_recv, dxp_send, dxp_recv,
    dx_send, dx_recv, k1_send, k1_recv, k2_send, k2_recv, k3_send, k3_recv, o_sem,
):
    dp, tm = lax.axis_index("dp"), lax.axis_index("tm")
    xl, y = lax.div(dp, 4), lax.rem(dp, 4)
    xh, z, c = lax.div(tm, 16), lax.rem(lax.div(tm, 2), 8), lax.rem(tm, 2)
    primary = c == xl
    inv = 1.0 / math.sqrt(POSITIONS)

    def dev(xl_, y_, xh_, z_, c_):
        return (xl_ * 4 + y_, (xh_ * 8 + z_) * 2 + c_)

    def remote(src, dst, send, recv, device):
        return pltpu.make_async_remote_copy(
            src_ref=src, dst_ref=dst, send_sem=send, recv_sem=recv, device_id=device, device_id_type=MESH
        )

    def landed(dst, sem):
        pltpu.make_async_copy(dst, dst, sem).wait()

    def plus(a, by, n):
        return lax.rem(a + by, n)

    partner = dev(1 - xl, y, xh, z, c)
    sibling = dev(xl, y, xh, z, 1 - c)
    across = dev(xl, y, 1 - xh, z, c)

    x_in = pltpu.make_async_copy(x_ref, xv, v_sem.at[0])
    x_in.start()

    barrier = pltpu.get_barrier_semaphore()
    peers = [partner]
    for dz in range(8):
        for dc in range(2):
            if dz or dc:
                peers.append(dev(xl, y, xh, plus(z, dz, 8), plus(c, dc, 2)))
    for dy in range(4):
        for dh in range(2):
            for dc in range(2):
                if dy or dh:
                    peers.append(dev(xl, plus(y, dy, 4), plus(xh, dh, 2), z, plus(c, dc, 2)))
    for dz in range(1, 8):
        peers.append(dev(xl, y, 1 - xh, plus(z, dz, 8), c))
    for peer in peers:
        pl.semaphore_signal(barrier, inc=1, device_id=peer, device_id_type=MESH)

    biasb[...] = jnp.broadcast_to(bias_ref[...], (8, 128))
    x_in.wait()
    for zt in range(8):
        at = (zt // 2) * 128 + (zt % 2) * 64
        xp[zt] = jnp.concatenate([xv[:, at:at + 64], xv[:, 512 + at:512 + at + 64]], axis=1)
    pl.semaphore_wait(barrier, len(peers))

    ends = []

    me_k = 2 * z + c
    for n, dz in enumerate((1, 7, 2, 6, 3, 5, 4)):
        zt = plus(z, dz, 8)
        copy = remote(xp.at[zt], land.at[me_k], x_send.at[n], x_recv.at[me_k], dev(xl, y, xh, zt, xl))
        copy.start()
        ends.append(copy.wait_send)
    own_x = pltpu.make_async_copy(xp.at[z], land.at[me_k], x_recv.at[me_k])
    sib_x = remote(xp.at[z], land.at[me_k], x_send.at[7], x_recv.at[me_k], dev(xl, y, xh, z, 1 - c))

    @pl.when(primary)
    def _():
        own_x.start()

    @pl.when(jnp.logical_not(primary))
    def _():
        sib_x.start()

    def w_at(h_, c_, y_):
        return wg.at[:, pl.ds(pl.multiple_of((h_ * 2 + c_) * 32, 32), 32), pl.ds(pl.multiple_of(y_ * 128, 128), 128)]

    def w_sem(h_, c_, y_):
        return w_recv.at[(h_ * 2 + c_) * 4 + y_]

    w_count = [0]

    def w_push(src, h_, c_, y_, device):
        copy = remote(src, w_at(h_, c_, y_), w_send.at[w_count[0]], w_sem(h_, c_, y_), device)
        w_count[0] += 1
        copy.start()
        ends.append(copy.wait_send)

    up, down = plus(y, 1, 4), plus(y, 3, 4)
    dev_up, dev_down = dev(xl, up, xh, z, c), dev(xl, down, xh, z, c)
    w_push(w_ref, xh, c, y, across)
    w_push(w_ref, xh, c, y, dev_up)
    w_push(w_ref, xh, c, y, dev_down)
    w_push(w_ref, xh, c, y, sibling)
    pltpu.make_async_copy(w_ref, w_at(xh, c, y), w_sem(xh, c, y)).start()

    for dy in range(4):
        for dc in range(2):
            yd, cd = plus(y, dy, 4), plus(c, dc, 2)
            src, dst, sem = cot_ref.at[cd * 4 + yd], cotl.at[c, y], c_recv.at[c * 4 + y]
            if dy or dc:
                copy = remote(src, dst, c_send.at[dy * 2 + dc], sem, dev(xl, yd, xh, z, cd))
                copy.start()
                ends.append(copy.wait_send)
            else:
                pltpu.make_async_copy(src, dst, sem).start()
    pltpu.make_async_copy(biasb, biasl.at[y], b_recv.at[y]).start()
    for dy in range(1, 4):
        copy = remote(biasb, biasl.at[y], b_send.at[dy], b_recv.at[y], dev(xl, plus(y, dy, 4), xh, z, c))
        copy.start()
        ends.append(copy.wait_send)

    halo_copy = remote(land.at[15, pl.ds(288, 96)], halo, h_sem.at[0], h_sem.at[1], across)
    ends.append(halo_copy.wait_send)

    def spread(j, carry):
        dz = jnp.where(lax.rem(j, 2) == 1, lax.div(j + 1, 2), lax.rem(8 - lax.div(j, 2), 8))
        zs = plus(z, dz, 8)
        for cs in range(2):
            k = 2 * zs + cs
            landed(land.at[k], x_recv.at[k])

            @pl.when(primary)
            def _():
                remote(land.at[k], land.at[k], f_send.at[k], x_recv.at[k], partner).start()

            if cs == 1:
                @pl.when(k == 15)
                def _():
                    halo_copy.start()

        for cs in range(2):
            k = 2 * zs + cs
            frames = land[k]
            side = jnp.concatenate([frames[i * 96:(i + 1) * 96] for i in range(4)], axis=1)
            taps = jnp.dot(gat_ref[...], side, preferred_element_type=F32)
            for i in range(4):
                piece = taps[:216, i * 128:(i + 1) * 128].reshape(9, 24, 128)
                if i % 2 == 0:
                    im_e[:, 2 * k + i // 2] = piece
                else:
                    im_o[:, 2 * k + 1 + i // 2] = piece
        return carry

    def w_pass(h_, y_, device):
        landed(w_at(h_, c, y_), w_sem(h_, c, y_))
        if device is not None:
            w_push(w_at(h_, c, y_), h_, c, y_, device)
        w_push(w_at(h_, c, y_), h_, c, y_, sibling)

    lax.fori_loop(0, 2, spread, 0)
    w_pass(1 - xh, y, dev_up)
    w_push(w_at(1 - xh, c, y), 1 - xh, c, y, dev_down)
    lax.fori_loop(2, 3, spread, 0)
    w_pass(xh, down, dev_up)
    w_pass(xh, up, None)
    lax.fori_loop(3, 5, spread, 0)
    w_pass(1 - xh, up, dev_down)
    w_pass(1 - xh, down, None)
    lax.fori_loop(5, 8, spread, 0)
    w_pass(xh, plus(y, 2, 4), None)
    w_pass(1 - xh, plus(y, 2, 4), None)
    landed(w_at(xh, c, y), w_sem(xh, c, y))
    for dy in range(4):
        for h_ in (xh, 1 - xh):
            yd = plus(y, dy, 4)
            landed(w_at(h_, 1 - c, yd), w_sem(h_, 1 - c, yd))

    landed(halo, h_sem.at[1])
    rim = jnp.dot(gat_ref[...], halo[...], preferred_element_type=F32)[:216].reshape(9, 24, 128)
    im_o[:, 0] = jnp.where(xh == 1, rim, jnp.zeros_like(rim))

    def forward(dzs):
        zts = [plus(z, dz, 8) for dz in dzs]

        def rows(held, hw, by):
            return jnp.concatenate([held[hw, pl.ds(4 * zt + by, 4)].reshape(96, 128) for zt in zts], axis=0).astype(BF16)

        def step(h, carry):
            lhs, rhs = [], []
            for w in range(3):
                hw = h * 3 + w
                lhs += [rows(im_o, hw, 0), rows(im_e, hw, 0), rows(im_o, hw, 1)]
                rhs += [wg[hw], wg[9 + hw], wg[18 + hw]]
            pacc[...] += jnp.dot(
                jnp.concatenate(lhs, axis=1), jnp.concatenate(rhs, axis=0), preferred_element_type=F32
            )
            return carry

        pacc[...] = jnp.zeros_like(pacc)
        lax.fori_loop(0, 3, step, 0)
        for q in range(4):
            zt = zts[q]
            part[zt] = pacc[q * 96:(q + 1) * 96].astype(BF16)
            if dzs[q]:
                copy = remote(part.at[zt], rsl.at[z], rs_send.at[dzs[q]], rs_recv.at[z], dev(xl, y, xh, zt, c))
                copy.start()
                ends.append(copy.wait_send)

    forward((4, 3, 5, 2))
    forward((6, 1, 7, 0))

    for dy in range(4):
        yd = plus(y, dy, 4)
        landed(biasl.at[yd], b_recv.at[yd])
        for cs in range(2):
            landed(cotl.at[cs, yd], c_recv.at[cs * 4 + yd])
    pre = part[z].astype(F32)
    for dz in (1, 7, 2, 6, 3, 5, 4):
        zs = plus(z, dz, 8)
        landed(rsl.at[zs], rs_recv.at[zs])
        pre = pre + rsl[zs].astype(F32)
    pre = pre + jnp.concatenate([biasl[i, 0:1] for i in range(4)], axis=1)
    sig = 1.0 / (1.0 + jnp.exp(-pre))
    samp = (pre * sig).astype(BF16)
    cot = jnp.concatenate(
        [jnp.concatenate([cotl[cs, i] for i in range(4)], axis=1) for cs in range(2)], axis=0
    ).astype(F32)
    slope = cot * sig * (1.0 + pre * (1.0 - sig))
    gbuf[z] = slope.astype(BF16)
    def g_at(o, half):
        return gbuf.at[o, pl.ds(half * 48, 48)]

    ag_count = [0]

    def ag_push(o, half, device):
        copy = remote(g_at(o, half), g_at(o, half), ag_send.at[ag_count[0]], ag_recv.at[o * 2 + half], device)
        ag_count[0] += 1
        copy.start()
        ends.append(copy.wait_send)

    next_z, last_z = dev(xl, y, xh, plus(z, 1, 8), c), dev(xl, y, xh, plus(z, 7, 8), c)
    for half in range(2):
        ag_push(z, half, next_z)
        ag_push(z, half, last_z)

    def rim_copy(zt):
        return remote(
            gbuf.at[0, pl.ds(0, 32)], gbuf.at[8, pl.ds(0, 32)], gh_send.at[zt], gh_recv.at[0], dev(xl, y, 0, zt, c)
        )

    gives_rim = jnp.logical_and(z == 0, xh == 1)

    @pl.when(gives_rim)
    def _():
        for zt in range(8):
            rim_copy(zt).start()

    @pl.when(xh == 1)
    def _():
        gbuf[8, pl.ds(0, 32)] = jnp.zeros((32, 512), BF16)

    sums = jnp.sum(slope, axis=0, keepdims=True)
    bz[z] = jnp.concatenate([sums[:, i * 128:(i + 1) * 128] for i in range(4)] + [jnp.zeros((4, 128), F32)], axis=0)
    for n, dz in enumerate((1, 7, 2, 6, 3, 5, 4)):
        copy = remote(bz.at[z], bz.at[z], bz_send.at[n], bz_recv.at[z], dev(xl, y, xh, plus(z, dz, 8), c))
        copy.start()
        ends.append(copy.wait_send)
    for cs in range(2):
        for i in range(4):
            sbuf[cs, i] = samp[cs * 48:(cs + 1) * 48, i * 128:(i + 1) * 128]
    for dy in range(4):
        for dc in range(2):
            yd, cd = plus(y, dy, 4), plus(c, dc, 2)
            src, dst, sem = sbuf.at[cd, yd], sland.at[c * 4 + y], s_recv.at[c * 4 + y]
            if dy or dc:
                copy = remote(src, dst, s_send.at[dy * 2 + dc], sem, dev(xl, yd, xh, z, cd))
                copy.start()
                ends.append(copy.wait_send)
            else:
                pltpu.make_async_copy(src, dst, sem).start()

    def chunk_back(zc):
        def back(h, carry):
            hws = [h * 3 + w for w in range(3)]
            mats = jnp.concatenate([wg[t * 9 + hw] for hw in hws for t in range(3)], axis=0)
            rows = jnp.concatenate([gbuf[zc], gbuf[zc + 1, 0:32]], axis=0)
            r = lax.dot_general(rows, mats, (((1,), (1,)), ((), ())), preferred_element_type=F32)
            for w in range(3):
                at = w * 384
                dtmp[h * 3 + w, 0:4] = r[:96, at + 128:at + 256].reshape(4, 24, 128)
                dtmp[h * 3 + w, 4:8] = (r[:96, at + 256:at + 384] + r[24:120, at:at + 128]).reshape(4, 24, 128)
            return carry

        lax.fori_loop(0, 3, back, 0)
        cols = [dtmp[:, i + 4 * odd].reshape(216, 128) for i in range(4) for odd in range(2)]
        side = jnp.concatenate(cols, axis=1)
        side = jnp.concatenate([side, jnp.zeros((8, 1024), F32)], axis=0).astype(BF16)
        r = jnp.dot(sca_ref[...], side, preferred_element_type=F32).astype(BF16)
        for cs in range(2):
            k = 2 * zc + cs
            for i in range(4):
                dxb[k, pl.ds(i * 96, 96)] = r[:, (cs * 4 + i) * 128:(cs * 4 + i + 1) * 128]

            @pl.when(jnp.logical_not(primary))
            def _(k=k):
                remote(dxb.at[k], dxp.at[k], dxp_send.at[k], dxp_recv.at[k], partner).start()

    def back_pair(first, second):
        def one(i, carry):
            chunk_back(jnp.where(i == 0, first, second))
            return carry

        lax.fori_loop(0, 2, one, 0)

    def send_back(k):
        landed(dxp.at[k], dxp_recv.at[k])
        dxs[k] = (dxb[k].astype(F32) + dxp[k].astype(F32)).astype(BF16)

        @pl.when(k == me_k)
        def _():
            pltpu.make_async_copy(dxs.at[k], dxl.at[z], dx_recv.at[z]).start()

        @pl.when(k != me_k)
        def _():
            remote(
                dxs.at[k], dxl.at[z], dx_send.at[k], dx_recv.at[z], dev(xl, y, xh, lax.div(k, 2), lax.rem(k, 2))
            ).start()

    def finish_pair(first, second):
        @pl.when(primary)
        def _():
            def one(i, carry):
                zc = jnp.where(i < 2, first, second)
                send_back(2 * zc + lax.rem(i, 2))
                return carry

            lax.fori_loop(0, 4, one, 0)

    def z_at(dz):
        return plus(z, dz % 8, 8)

    for step in range(1, 4):
        below, above = z_at(-step), z_at(step)
        for half in range(2):
            landed(g_at(below, half), ag_recv.at[below * 2 + half])
            if step < 3 or half == 0:
                ag_push(below, half, next_z)
            landed(g_at(above, half), ag_recv.at[above * 2 + half])
            if step < 3 or half == 1:
                ag_push(above, half, last_z)
        if step == 1:
            @pl.when(xh == 0)
            def _():
                landed(gbuf.at[8, pl.ds(0, 32)], gh_recv.at[0])

        back_pair(z_at(step - 1), z_at(-step))
        if step > 1:
            finish_pair(z_at(step - 2), z_at(1 - step))
    for half in range(2):
        landed(g_at(z_at(4), half), ag_recv.at[z_at(4) * 2 + half])

    def weight_grad(h):
        def grad_step(w, carry):
            hw = h * 3 + w
            lhs = jnp.concatenate(
                [
                    im_o[hw, pl.ds(0, 32)].reshape(768, 128).astype(BF16),
                    im_e[hw].reshape(768, 128).astype(BF16),
                    im_o[hw, pl.ds(1, 32)].reshape(768, 128).astype(BF16),
                ],
                axis=1,
            )
            r = lax.dot_general(
                lhs, gbuf[0:8].reshape(768, 512), (((0,), (0,)), ((), ())), preferred_element_type=F32
            ).astype(BF16)
            for t in range(3):
                for h_ in range(2):
                    for c_ in range(2):
                        at = t * 128 + h_ * 64 + c_ * 32
                        dwb[h, c_, h_, w * 3 + t] = r[at:at + 32]
            return carry

        lax.fori_loop(0, 3, grad_step, 0)
        copy = remote(dwb.at[h, 1 - c], dws.at[h], k1_send.at[h], k1_recv.at[h], sibling)
        copy.start()
        ends.append(copy.wait_send)

    def over_y(h):
        landed(dws.at[h], k1_recv.at[h])

        def add_step(n, carry):
            for h_ in range(2):
                dwr[h, h_, n] = (dwb[h, c, h_, n].astype(F32) + dws[h, h_, n].astype(F32)).astype(BF16)
            return carry

        lax.fori_loop(0, 9, add_step, 0)
        for dy in range(4):
            yd = plus(y, dy, 4)
            src = dwr.at[h, :, :, :, pl.ds(pl.multiple_of(yd * 128, 128), 128)]
            dst, sem = dwl.at[h, y], k2_recv.at[h * 4 + y]
            if dy:
                copy = remote(src, dst, k2_send.at[h * 4 + dy], sem, dev(xl, yd, xh, z, c))
                copy.start()
                ends.append(copy.wait_send)
            else:
                pltpu.make_async_copy(src, dst, sem).start()

    def over_x(h):
        for i in range(4):
            landed(dwl.at[h, i], k2_recv.at[h * 4 + i])

        def add_step(n, carry):
            own, other = dwl[h, 0, xh, n].astype(F32), dwl[h, 0, 1 - xh, n].astype(F32)
            for i in range(1, 4):
                own = own + dwl[h, i, xh, n].astype(F32)
                other = other + dwl[h, i, 1 - xh, n].astype(F32)
            dwo[h, n] = own
            dwx[h, n] = other.astype(BF16)
            return carry

        lax.fori_loop(0, 9, add_step, 0)
        copy = remote(dwx.at[h], dwy.at[h], k3_send.at[h], k3_recv.at[h], across)
        copy.start()
        ends.append(copy.wait_send)

    weight_grad(0)
    back_pair(z_at(3), z_at(4))
    over_y(0)
    finish_pair(z_at(2), z_at(-3))
    weight_grad(1)
    weight_grad(2)
    over_y(1)
    finish_pair(z_at(3), z_at(4))
    over_y(2)

    total = bz[z]
    for dz in (1, 7, 2, 6, 3, 5, 4):
        zs = plus(z, dz, 8)
        landed(bz.at[zs], bz_recv.at[zs])
        total = total + bz[zs]
    for i in range(4):
        bs[i] = jnp.broadcast_to(total[i:i + 1], (8, 128))
    slot_b = (xh * 2 + c) * 4 + y
    for dy in range(4):
        for dh in range(2):
            for dc in range(2):
                yd, hd, cd = plus(y, dy, 4), plus(xh, dh, 2), plus(c, dc, 2)
                if dy or dh or dc:
                    copy = remote(
                        bs.at[yd], bl.at[slot_b], bs_send.at[(dy * 2 + dh) * 2 + dc], bs_recv.at[slot_b],
                        dev(xl, yd, hd, z, cd),
                    )
                    copy.start()
                    ends.append(copy.wait_send)
                else:
                    pltpu.make_async_copy(bs.at[y], bl.at[slot_b], bs_recv.at[slot_b]).start()

    outs = []
    for i in range(8):
        landed(sland.at[i], s_recv.at[i])
    outs.append(pltpu.make_async_copy(sland, samp_out, o_sem.at[0]))
    outs[-1].start()

    for h in range(3):
        over_x(h)
    for h in range(3):
        landed(dwy.at[h], k3_recv.at[h])

        def sum_step(w, carry, h=h):
            for t in range(3):
                kout[t * 9 + h * 3 + w] = (dwo[h, w * 3 + t] + dwy[h, w * 3 + t].astype(F32)) * inv
            return carry

        lax.fori_loop(0, 3, sum_step, 0)
    outs.append(pltpu.make_async_copy(kout, dw_out, o_sem.at[1]))
    outs[-1].start()

    acc = None
    for i in range(16):
        landed(bl.at[i], bs_recv.at[i])
        acc = bl[i] if acc is None else acc + bl[i]
    dbo[...] = acc[0:1] * inv
    outs.append(pltpu.make_async_copy(dbo, db_out, o_sem.at[2]))
    outs[-1].start()

    for m in range(4):
        for i in (2 * m, 2 * m + 1):
            landed(dxl.at[i], dx_recv.at[i])
        a, b = dxl[2 * m], dxl[2 * m + 1]
        dxo[:, m * 128:(m + 1) * 128] = jnp.concatenate([a[:, :64], b[:, :64]], axis=1)
        dxo[:, 512 + m * 128:512 + (m + 1) * 128] = jnp.concatenate([a[:, 64:], b[:, 64:]], axis=1)
    outs.append(pltpu.make_async_copy(dxo, dx_out, o_sem.at[3]))
    outs[-1].start()

    for end in ends:
        end()

    @pl.when(jnp.logical_not(primary))
    def _():
        sib_x.wait_send()

        def drain(k, carry):
            remote(dxb.at[k], dxp.at[k], dxp_send.at[k], dxp_recv.at[k], partner).wait_send()
            return carry

        lax.fori_loop(0, 16, drain, 0)

    @pl.when(primary)
    def _():
        def drain(k, carry):
            remote(land.at[k], land.at[k], f_send.at[k], x_recv.at[k], partner).wait_send()

            @pl.when(k != me_k)
            def _():
                remote(
                    dxs.at[k], dxl.at[z], dx_send.at[k], dx_recv.at[z],
                    dev(xl, y, xh, lax.div(k, 2), lax.rem(k, 2)),
                ).wait_send()

            return carry

        lax.fori_loop(0, 16, drain, 0)

    @pl.when(gives_rim)
    def _():
        for zt in range(8):
            rim_copy(zt).wait_send()

    for out in outs:
        out.wait()


def shards(video_clips, weights, conv_bias, cotangent):
    x = video_clips.reshape(384, 1024)
    w = weights.reshape(27, 32, 128)
    cot = cotangent.transpose(0, 1, 3, 2, 4).reshape(8, 48, 128)
    bias = conv_bias.reshape(1, 128)
    table = tap_gather()
    gat = jnp.asarray(table, BF16)
    sca = jnp.asarray(table.T, BF16)
    any_spec = pl.BlockSpec(memory_space=pl.ANY)
    vmem_spec = pl.BlockSpec(memory_space=pltpu.VMEM)

    def v(shape, dtype=BF16):
        return pltpu.VMEM(shape, dtype)

    def sems(n):
        return pltpu.SemaphoreType.DMA((n,))

    samp, dx, dw, db = pl.pallas_call(
        kernel,
        out_shape=[
            jax.ShapeDtypeStruct((8, 48, 128), BF16),
            jax.ShapeDtypeStruct((384, 1024), BF16),
            jax.ShapeDtypeStruct((27, 32, 128), F32),
            jax.ShapeDtypeStruct((1, 128), F32),
        ],
        in_specs=[any_spec] * 3 + [vmem_spec] * 3,
        out_specs=[any_spec] * 4,
        scratch_shapes=[
            v((384, 1024)),
            v((8, 384, 128)),
            v((16, 384, 128)),
            v((96, 128)),
            v((27, 128, 512)),
            v((2, 4, 48, 128)),
            v((8, 128), F32),
            v((4, 8, 128), F32),
            v((9, 32, 24, 128), F32),
            v((9, 33, 24, 128), F32),
            v((384, 512), F32),
            v((8, 96, 512)),
            v((8, 96, 512)),
            v((2, 4, 48, 128)),
            v((8, 48, 128)),
            v((9, 96, 512)),
            v((8, 8, 128), F32),
            v((4, 8, 128), F32),
            v((16, 8, 128), F32),
            v((9, 8, 24, 128), F32),
            v((16, 384, 128)),
            v((16, 384, 128)),
            v((16, 384, 128)),
            v((8, 384, 128)),
            v((384, 1024)),
            v((3, 2, 2, 9, 32, 512)),
            v((3, 2, 9, 32, 512)),
            v((3, 2, 9, 32, 512)),
            v((3, 4, 2, 9, 32, 128)),
            v((3, 9, 32, 128), F32),
            v((3, 9, 32, 128)),
            v((3, 9, 32, 128)),
            v((27, 32, 128), F32),
            v((1, 128), F32),
            sems(1), sems(8), sems(16), sems(16), sems(2),
            sems(16), sems(16), sems(8), sems(8), sems(4), sems(4),
            sems(8), sems(8), sems(8), sems(8), sems(14), sems(16), sems(8), sems(8),
            sems(8), sems(1), sems(16), sems(16), sems(16), sems(16), sems(16), sems(8),
            sems(3), sems(3), sems(12), sems(12), sems(3), sems(3), sems(4),
        ],
        compiler_params=pltpu.CompilerParams(
            collective_id=0, has_side_effects=True, vmem_limit_bytes=60 * 1024 * 1024
        ),
        cost_estimate=pl.CostEstimate(flops=10_000_000_000, bytes_accessed=8_000_000, transcendentals=50_000),
    )(x, w, cot, bias, gat, sca)
    sampled = samp.reshape(8, 2, 12, 2, 128).transpose(0, 1, 3, 2, 4)
    clip_grad = dx.reshape(1, 4, 4, 24, 1024)
    return sampled, clip_grad, dw.reshape(3, 3, 3, 32, 128), db.reshape(128)


def solution(mesh):
    return jax.shard_map(
        shards,
        mesh=mesh,
        in_specs=(
            P("dp", "tm", None, None, None),
            P(None, None, None, "tm", "dp"),
            P("dp"),
            P(None, "tm", None, None, "dp"),
        ),
        out_specs=(
            P(None, "tm", None, None, "dp"),
            P("dp", "tm", None, None, None),
            P(None, None, None, "tm", "dp"),
            P("dp"),
        ),
        check_vma=False,
    )
```

time: 150 us -> 119 us (0.79)
  the two profiles are of different devices: /device:TPU:7 before, /device:TPU:102 now
where the time goes in v2:
time: 119 us
  Pallas kernels  114 us (96%)
  local copies, waits for them, and re-layouts  5.02 us (4%)
    pallas_call x1, Pallas kernels, shards(): pl.pallas_call(kernel, out_shape=[jax.ShapeDtypeStruct((8, 48, 128), BF16...  114 us
    unnamed x8, local copies, waits for them, and re-layouts  5.02 us

profile of v2, /device:TPU:102, one launch (start us, length us, event | category | flops | bytes accessed | tf_op | source)
XLA Modules:
  0.0 119.2 jit_solution(2690910398002040255)
XLA Ops:
  0.6 113.6 %shard_map.93 = (bf16[8,48,128]{2,1,0:T(8,128)(2,1)}, bf16[384,1024]{1,0:T(8,128)(2,1)}, f32[27,32,128]{2,1,0:T(8,128)}, f32[1,128]{1,0:T(1,128)}) custom-call(bf16[384,1024]{1,0:T(8,128)(2,1)} %bitcast.15, bf16[27,32,128]{2,1,0:T(8,128)(2,1)} %bitcast.16, bf16[8,48,128]{2,1,0:T(8,128)(2,1)} %bitcast.17, f32[1,128]{1,0:T(1,128)} %bitcast.18, ...), custom_call_target="tpu_custom_call" | custom-call | flops 10000000000 | bytes 8000000 | tf_op jit(solution)/shard_map/pallas_call | solution.py:573
  114.2 1.6 %copy.14 = bf16[8,2,2,12,128]{4,2,3,1,0:T(2,128)(2,1)} copy(bf16[8,2,2,12,128]{4,2,3,1,0:T(2,128)(2,1)} %bitcast.14) | data formatting | bytes 196608
  115.8 0.0 copy-start
  115.8 2.1 %copy.15 = bf16[1,4,4,24,1024]{4,3,2,1,0:T(8,128)(2,1)} copy(bf16[1,4,4,24,1024]{4,3,2,1,0:T(8,128)(2,1)} %bitcast.12) | data formatting | bytes 1572864
  117.9 0.0 copy-done
  117.9 0.0 copy-start.1
  117.9 0.8 copy.16
  118.7 0.0 copy-done.1
  118.7 0.5 copy.17
Async XLA Ops:
  115.8 2.1 %copy-start = (f32[27,32,128]{2,1,0:T(8,128)S(1)}, f32[27,32,128]{2,1,0:T(8,128)}, u32[]{:S(2)}) copy-start(f32[27,32,128]{2,1,0:T(8,128)} %get-tuple-element.10) | copy-start | bytes 1327108
  117.9 0.8 copy-start.1

commit v3 on v2

--- a/solution.py
+++ b/solution.py
@@ -29,8 +29,8 @@
 def kernel(
     x_ref, w_ref, cot_ref, bias_ref, gat_ref, sca_ref,
     samp_out, dx_out, dw_out, db_out,
-    xv, xp, land, halo, wg, cotl, biasb, biasl, im_e, im_o, pacc, part, rsl, sbuf, sland, gbuf, bz, bs, bl,
-    dtmp, dxb, dxp, dxs, dxl, dxo, dwb, dws, dwr, dwl, dwo, dwx, dwy, kout, dbo,
+    xv, xp, land, halo, wg, cotl, biasb, biasl, im_e, im_o, pacc, part, rsl, rss, sbuf, sland, gbuf, bz, bs, bl,
+    dtmp, dxb, dxp, dxs, dxl, dxo, dwb, dws, dwr, dwl, dwo, dwx, dwy, dwm, dwn, kout, dbo,
     v_sem, x_send, x_recv, f_send, h_sem, w_send, w_recv, c_send, c_recv, b_send, b_recv, rs_send, rs_recv,
     s_send, s_recv, ag_send, ag_recv, bz_send, bz_recv, gh_send, gh_recv, bs_send, bs_recv, dxp_send, dxp_recv,
     dx_send, dx_recv, k1_send, k1_recv, k2_send, k2_recv, k3_send, k3_recv, o_sem,
@@ -88,7 +88,7 @@
     ends = []
 
     me_k = 2 * z + c
-    for n, dz in enumerate((1, 7, 2, 6, 3, 5, 4)):
+    for n, dz in enumerate((4, 3, 5, 2, 6, 1, 7)):
         zt = plus(z, dz, 8)
         copy = remote(xp.at[zt], land.at[me_k], x_send.at[n], x_recv.at[me_k], dev(xl, y, xh, zt, xl))
         copy.start()
@@ -145,34 +145,49 @@
     halo_copy = remote(land.at[15, pl.ds(288, 96)], halo, h_sem.at[0], h_sem.at[1], across)
     ends.append(halo_copy.wait_send)
 
-    def spread(j, carry):
-        dz = jnp.where(lax.rem(j, 2) == 1, lax.div(j + 1, 2), lax.rem(8 - lax.div(j, 2), 8))
-        zs = plus(z, dz, 8)
-        for cs in range(2):
-            k = 2 * zs + cs
-            landed(land.at[k], x_recv.at[k])
-
-            @pl.when(primary)
+    def place_of(j):
+        far = jnp.where(lax.rem(j, 2) == 0, 4 - lax.div(j, 2), 4 + lax.div(j, 2))
+        return plus(z, jnp.where(j == 0, 0, far), 8)
+
+    def pass_on(first, last):
+        @pl.when(primary)
+        def _():
+            def one(i, carry):
+                k = 2 * place_of(lax.div(i, 2)) + lax.rem(i, 2)
+                landed(land.at[k], x_recv.at[k])
+                remote(land.at[k], land.at[k], f_send.at[k], x_recv.at[k], partner).start()
+                return carry
+
+            lax.fori_loop(2 * first, 2 * last, one, 0)
+
+    def take_in(first, last):
+        def one(i, carry):
+            k = 2 * place_of(lax.div(i, 2)) + lax.rem(i, 2)
+
+            @pl.when(jnp.logical_not(primary))
             def _():
-                remote(land.at[k], land.at[k], f_send.at[k], x_recv.at[k], partner).start()
-
-            if cs == 1:
-                @pl.when(k == 15)
-                def _():
-                    halo_copy.start()
-
-        for cs in range(2):
-            k = 2 * zs + cs
+                landed(land.at[k], x_recv.at[k])
+
+            @pl.when(k == 15)
+            def _():
+                halo_copy.start()
+
             frames = land[k]
             side = jnp.concatenate([frames[i * 96:(i + 1) * 96] for i in range(4)], axis=1)
             taps = jnp.dot(gat_ref[...], side, preferred_element_type=F32)
-            for i in range(4):
-                piece = taps[:216, i * 128:(i + 1) * 128].reshape(9, 24, 128)
-                if i % 2 == 0:
-                    im_e[:, 2 * k + i // 2] = piece
+            for f in range(4):
+                piece = taps[:216, f * 128:(f + 1) * 128].reshape(9, 24, 128)
+                if f % 2 == 0:
+                    im_e[:, 2 * k + f // 2] = piece
                 else:
-                    im_o[:, 2 * k + 1 + i // 2] = piece
-        return carry
+                    im_o[:, 2 * k + 1 + f // 2] = piece
+            return carry
+
+        lax.fori_loop(2 * first, 2 * last, one, 0)
+
+    def spread(first, last):
+        pass_on(first, last)
+        take_in(first, last)
 
     def w_pass(h_, y_, device):
         landed(w_at(h_, c, y_), w_sem(h_, c, y_))
@@ -180,16 +195,17 @@
             w_push(w_at(h_, c, y_), h_, c, y_, device)
         w_push(w_at(h_, c, y_), h_, c, y_, sibling)
 
-    lax.fori_loop(0, 2, spread, 0)
+    spread(0, 1)
     w_pass(1 - xh, y, dev_up)
     w_push(w_at(1 - xh, c, y), 1 - xh, c, y, dev_down)
-    lax.fori_loop(2, 3, spread, 0)
+    spread(1, 2)
     w_pass(xh, down, dev_up)
     w_pass(xh, up, None)
-    lax.fori_loop(3, 5, spread, 0)
+    spread(2, 4)
     w_pass(1 - xh, up, dev_down)
     w_pass(1 - xh, down, None)
-    lax.fori_loop(5, 8, spread, 0)
+    spread(4, 6)
+    pass_on(6, 8)
     w_pass(xh, plus(y, 2, 4), None)
     w_pass(1 - xh, plus(y, 2, 4), None)
     landed(w_at(xh, c, y), w_sem(xh, c, y))
@@ -198,12 +214,18 @@
             yd = plus(y, dy, 4)
             landed(w_at(h_, 1 - c, yd), w_sem(h_, 1 - c, yd))
 
-    landed(halo, h_sem.at[1])
-    rim = jnp.dot(gat_ref[...], halo[...], preferred_element_type=F32)[:216].reshape(9, 24, 128)
-    im_o[:, 0] = jnp.where(xh == 1, rim, jnp.zeros_like(rim))
+    def z_at(dz):
+        return plus(z, dz % 8, 8)
 
     def forward(dzs):
-        zts = [plus(z, dz, 8) for dz in dzs]
+        zts = [z_at(dz) for dz in dzs]
+        size = 96 * len(zts)
+        for zt in zts:
+            @pl.when(zt == 0)
+            def _():
+                landed(halo, h_sem.at[1])
+                rim = jnp.dot(gat_ref[...], halo[...], preferred_element_type=F32)[:216].reshape(9, 24, 128)
+                im_o[:, 0] = jnp.where(xh == 1, rim, jnp.zeros_like(rim))
 
         def rows(held, hw, by):
             return jnp.concatenate([held[hw, pl.ds(4 * zt + by, 4)].reshape(96, 128) for zt in zts], axis=0).astype(BF16)
@@ -214,23 +236,47 @@
                 hw = h * 3 + w
                 lhs += [rows(im_o, hw, 0), rows(im_e, hw, 0), rows(im_o, hw, 1)]
                 rhs += [wg[hw], wg[9 + hw], wg[18 + hw]]
-            pacc[...] += jnp.dot(
+            pacc[0:size] += jnp.dot(
                 jnp.concatenate(lhs, axis=1), jnp.concatenate(rhs, axis=0), preferred_element_type=F32
             )
             return carry
 
-        pacc[...] = jnp.zeros_like(pacc)
+        pacc[0:size] = jnp.zeros((size, 512), F32)
         lax.fori_loop(0, 3, step, 0)
-        for q in range(4):
+        for q, dz in enumerate(dzs):
             zt = zts[q]
             part[zt] = pacc[q * 96:(q + 1) * 96].astype(BF16)
-            if dzs[q]:
-                copy = remote(part.at[zt], rsl.at[z], rs_send.at[dzs[q]], rs_recv.at[z], dev(xl, y, xh, zt, c))
-                copy.start()
-                ends.append(copy.wait_send)
-
-    forward((4, 3, 5, 2))
-    forward((6, 1, 7, 0))
+
+    next_z, last_z = dev(xl, y, xh, plus(z, 1, 8), c), dev(xl, y, xh, plus(z, 7, 8), c)
+
+    def rs_hop(way, step, half):
+        zt = z_at((5 - step) * (1 - 2 * way))
+        at = (way * 4 + step - 1) * 2 + half
+        own = part[zt, half * 48:(half + 1) * 48]
+        if step > 1 and (step > 2 or half == way):
+            before = at - 2
+            landed(rsl.at[before], rs_recv.at[before])
+            own = (own.astype(F32) + rsl[before].astype(F32)).astype(BF16)
+        rss[at] = own
+        copy = remote(rss.at[at], rsl.at[at], rs_send.at[at], rs_recv.at[at], last_z if way else next_z)
+        copy.start()
+        ends.append(copy.wait_send)
+
+    def rs_step(step):
+        for half in range(2):
+            for way in range(2):
+                if step > 1 or half == way:
+                    rs_hop(way, step, half)
+
+    forward((4, -3))
+    rs_step(1)
+    forward((3, -2))
+    take_in(6, 8)
+    rs_step(2)
+    forward((2, -1, 1))
+    rs_step(3)
+    forward((0,))
+    rs_step(4)
 
     for dy in range(4):
         yd = plus(y, dy, 4)
@@ -238,10 +284,13 @@
         for cs in range(2):
             landed(cotl.at[cs, yd], c_recv.at[cs * 4 + yd])
     pre = part[z].astype(F32)
-    for dz in (1, 7, 2, 6, 3, 5, 4):
-        zs = plus(z, dz, 8)
-        landed(rsl.at[zs], rs_recv.at[zs])
-        pre = pre + rsl[zs].astype(F32)
+    sums_in = []
+    for way in range(2):
+        for half in range(2):
+            at = (way * 4 + 3) * 2 + half
+            landed(rsl.at[at], rs_recv.at[at])
+        sums_in.append(jnp.concatenate([rsl[way * 8 + 6], rsl[way * 8 + 7]], axis=0).astype(F32))
+    pre = pre + sums_in[0] + sums_in[1]
     pre = pre + jnp.concatenate([biasl[i, 0:1] for i in range(4)], axis=1)
     sig = 1.0 / (1.0 + jnp.exp(-pre))
     samp = (pre * sig).astype(BF16)
@@ -261,7 +310,6 @@
         copy.start()
         ends.append(copy.wait_send)
 
-    next_z, last_z = dev(xl, y, xh, plus(z, 1, 8), c), dev(xl, y, xh, plus(z, 7, 8), c)
     for half in range(2):
         ag_push(z, half, next_z)
         ag_push(z, half, last_z)
@@ -302,38 +350,41 @@
             else:
                 pltpu.make_async_copy(src, dst, sem).start()
 
-    def chunk_back(zc):
+    def back_pair(first, second):
         def back(h, carry):
             hws = [h * 3 + w for w in range(3)]
             mats = jnp.concatenate([wg[t * 9 + hw] for hw in hws for t in range(3)], axis=0)
-            rows = jnp.concatenate([gbuf[zc], gbuf[zc + 1, 0:32]], axis=0)
+            rows = jnp.concatenate(
+                [gbuf[first], gbuf[first + 1, 0:32], gbuf[second], gbuf[second + 1, 0:32]], axis=0
+            )
             r = lax.dot_general(rows, mats, (((1,), (1,)), ((), ())), preferred_element_type=F32)
             for w in range(3):
                 at = w * 384
-                dtmp[h * 3 + w, 0:4] = r[:96, at + 128:at + 256].reshape(4, 24, 128)
-                dtmp[h * 3 + w, 4:8] = (r[:96, at + 256:at + 384] + r[24:120, at:at + 128]).reshape(4, 24, 128)
+                for i in range(2):
+                    p = r[i * 128:i * 128 + 128]
+                    dtmp[i, h * 3 + w, 0:4] = p[:96, at + 128:at + 256].reshape(4, 24, 128)
+                    dtmp[i, h * 3 + w, 4:8] = (p[:96, at + 256:at + 384] + p[24:120, at:at + 128]).reshape(4, 24, 128)
             return carry
 
         lax.fori_loop(0, 3, back, 0)
-        cols = [dtmp[:, i + 4 * odd].reshape(216, 128) for i in range(4) for odd in range(2)]
-        side = jnp.concatenate(cols, axis=1)
-        side = jnp.concatenate([side, jnp.zeros((8, 1024), F32)], axis=0).astype(BF16)
-        r = jnp.dot(sca_ref[...], side, preferred_element_type=F32).astype(BF16)
-        for cs in range(2):
-            k = 2 * zc + cs
-            for i in range(4):
-                dxb[k, pl.ds(i * 96, 96)] = r[:, (cs * 4 + i) * 128:(cs * 4 + i + 1) * 128]
-
-            @pl.when(jnp.logical_not(primary))
-            def _(k=k):
-                remote(dxb.at[k], dxp.at[k], dxp_send.at[k], dxp_recv.at[k], partner).start()
-
-    def back_pair(first, second):
-        def one(i, carry):
-            chunk_back(jnp.where(i == 0, first, second))
-            return carry
-
-        lax.fori_loop(0, 2, one, 0)
+
+        def place(i, carry):
+            zc = jnp.where(i == 0, first, second)
+            cols = [dtmp[i, :, f + 4 * odd].reshape(216, 128) for f in range(4) for odd in range(2)]
+            side = jnp.concatenate(cols, axis=1)
+            side = jnp.concatenate([side, jnp.zeros((8, 1024), F32)], axis=0).astype(BF16)
+            r = jnp.dot(sca_ref[...], side, preferred_element_type=F32).astype(BF16)
+            for cs in range(2):
+                k = 2 * zc + cs
+                for f in range(4):
+                    dxb[k, pl.ds(f * 96, 96)] = r[:, (cs * 4 + f) * 128:(cs * 4 + f + 1) * 128]
+
+                @pl.when(jnp.logical_not(primary))
+                def _(k=k):
+                    remote(dxb.at[k], dxp.at[k], dxp_send.at[k], dxp_recv.at[k], partner).start()
+            return carry
+
+        lax.fori_loop(0, 2, place, 0)
 
     def send_back(k):
         landed(dxp.at[k], dxp_recv.at[k])
@@ -358,9 +409,6 @@
                 return carry
 
             lax.fori_loop(0, 4, one, 0)
-
-    def z_at(dz):
-        return plus(z, dz % 8, 8)
 
     for step in range(1, 4):
         below, above = z_at(-step), z_at(step)
@@ -408,7 +456,7 @@
         copy.start()
         ends.append(copy.wait_send)
 
-    def over_y(h):
+    def core_sum(h):
         landed(dws.at[h], k1_recv.at[h])
 
         def add_step(n, carry):
@@ -417,9 +465,15 @@
             return carry
 
         lax.fori_loop(0, 9, add_step, 0)
+
+    def y_lanes(i):
+        return pl.ds(pl.multiple_of(i * 128, 128), 128)
+
+    def to_y(h):
+        core_sum(h)
         for dy in range(4):
             yd = plus(y, dy, 4)
-            src = dwr.at[h, :, :, :, pl.ds(pl.multiple_of(yd * 128, 128), 128)]
+            src = dwr.at[h, :, :, :, y_lanes(yd)]
             dst, sem = dwl.at[h, y], k2_recv.at[h * 4 + y]
             if dy:
                 copy = remote(src, dst, k2_send.at[h * 4 + dy], sem, dev(xl, yd, xh, z, c))
@@ -428,7 +482,7 @@
             else:
                 pltpu.make_async_copy(src, dst, sem).start()
 
-    def over_x(h):
+    def y_to_x(h):
         for i in range(4):
             landed(dwl.at[h, i], k2_recv.at[h * 4 + i])
 
@@ -446,15 +500,41 @@
         copy.start()
         ends.append(copy.wait_send)
 
+    def to_x(h):
+        core_sum(h)
+        copy = remote(dwr.at[h, 1 - xh], dwm, k3_send.at[h], k3_recv.at[h], across)
+        copy.start()
+        ends.append(copy.wait_send)
+
+    def x_to_y(h):
+        landed(dwm, k3_recv.at[h])
+
+        def add_step(n, carry):
+            dwn[n] = (dwr[h, xh, n].astype(F32) + dwm[n].astype(F32)).astype(BF16)
+            return carry
+
+        lax.fori_loop(0, 9, add_step, 0)
+        for dy in range(4):
+            yd = plus(y, dy, 4)
+            src = dwn.at[:, :, y_lanes(yd)]
+            dst, sem = dwl.at[h, y, 0], k2_recv.at[h * 4 + y]
+            if dy:
+                copy = remote(src, dst, k2_send.at[h * 4 + dy], sem, dev(xl, yd, xh, z, c))
+                copy.start()
+                ends.append(copy.wait_send)
+            else:
+                pltpu.make_async_copy(src, dst, sem).start()
+
     weight_grad(0)
     back_pair(z_at(3), z_at(4))
-    over_y(0)
+    to_y(0)
     finish_pair(z_at(2), z_at(-3))
     weight_grad(1)
     weight_grad(2)
-    over_y(1)
     finish_pair(z_at(3), z_at(4))
-    over_y(2)
+    to_x(1)
+    to_y(2)
+    x_to_y(1)
 
     total = bz[z]
     for dz in (1, 7, 2, 6, 3, 5, 4):
@@ -484,9 +564,21 @@
     outs.append(pltpu.make_async_copy(sland, samp_out, o_sem.at[0]))
     outs[-1].start()
 
-    for h in range(3):
-        over_x(h)
-    for h in range(3):
+    y_to_x(0)
+    y_to_x(2)
+    for i in range(4):
+        landed(dwl.at[1, i, 0], k2_recv.at[4 + i])
+
+    def sum_middle(w, carry):
+        for t in range(3):
+            acc = dwl[1, 0, 0, w * 3 + t].astype(F32)
+            for i in range(1, 4):
+                acc = acc + dwl[1, i, 0, w * 3 + t].astype(F32)
+            kout[t * 9 + 3 + w] = acc * inv
+        return carry
+
+    lax.fori_loop(0, 3, sum_middle, 0)
+    for h in (0, 2):
         landed(dwy.at[h], k3_recv.at[h])
 
         def sum_step(w, carry, h=h):
@@ -593,14 +685,15 @@
             v((9, 33, 24, 128), F32),
             v((384, 512), F32),
             v((8, 96, 512)),
-            v((8, 96, 512)),
+            v((16, 48, 512)),
+            v((16, 48, 512)),
             v((2, 4, 48, 128)),
             v((8, 48, 128)),
             v((9, 96, 512)),
             v((8, 8, 128), F32),
             v((4, 8, 128), F32),
             v((16, 8, 128), F32),
-            v((9, 8, 24, 128), F32),
+            v((2, 9, 8, 24, 128), F32),
             v((16, 384, 128)),
             v((16, 384, 128)),
             v((16, 384, 128)),
@@ -613,11 +706,13 @@
             v((3, 9, 32, 128), F32),
             v((3, 9, 32, 128)),
             v((3, 9, 32, 128)),
+            v((9, 32, 512)),
+            v((9, 32, 512)),
             v((27, 32, 128), F32),
             v((1, 128), F32),
             sems(1), sems(8), sems(16), sems(16), sems(2),
             sems(16), sems(16), sems(8), sems(8), sems(4), sems(4),
-            sems(8), sems(8), sems(8), sems(8), sems(14), sems(16), sems(8), sems(8),
+            sems(16), sems(16), sems(8), sems(8), sems(14), sems(16), sems(8), sems(8),
             sems(8), sems(1), sems(16), sems(16), sems(16), sems(16), sems(16), sems(8),
             sems(3), sems(3), sems(12), sems(12), sems(3), sems(3), sems(4),
         ],

time: 119 us -> 113 us (0.950)
  the two profiles are of different devices: /device:TPU:102 before, /device:TPU:97 now
where the time goes in v3:
time: 113 us; the launch traced here: 112 us
  Pallas kernels  106 us (94%)
  local copies, waits for them, and re-layouts  5.02 us (4%)
    pallas_call x1, Pallas kernels, shards(): pl.pallas_call(kernel, out_shape=[jax.ShapeDtypeStruct((8, 48, 128), BF16...  106 us
    unnamed x8, local copies, waits for them, and re-layouts  5.02 us

profile of v3, /device:TPU:97, one launch (start us, length us, event | category | flops | bytes accessed | tf_op | source)
XLA Modules:
  0.0 111.8 jit_solution(7298326369981832903)
XLA Ops:
  0.6 106.1 %shard_map.93 = (bf16[8,48,128]{2,1,0:T(8,128)(2,1)}, bf16[384,1024]{1,0:T(8,128)(2,1)}, f32[27,32,128]{2,1,0:T(8,128)}, f32[1,128]{1,0:T(1,128)}) custom-call(bf16[384,1024]{1,0:T(8,128)(2,1)} %bitcast.15, bf16[27,32,128]{2,1,0:T(8,128)(2,1)} %bitcast.16, bf16[8,48,128]{2,1,0:T(8,128)(2,1)} %bitcast.17, f32[1,128]{1,0:T(1,128)} %bitcast.18, ...), custom_call_target="tpu_custom_call" | custom-call | flops 10000000000 | bytes 8000000 | tf_op jit(solution)/shard_map/pallas_call | solution.py:665
  106.8 1.6 %copy.14 = bf16[8,2,2,12,128]{4,2,3,1,0:T(2,128)(2,1)} copy(bf16[8,2,2,12,128]{4,2,3,1,0:T(2,128)(2,1)} %bitcast.14) | data formatting | bytes 196608
  108.4 0.0 copy-start
  108.4 2.1 %copy.15 = bf16[1,4,4,24,1024]{4,3,2,1,0:T(8,128)(2,1)} copy(bf16[1,4,4,24,1024]{4,3,2,1,0:T(8,128)(2,1)} %bitcast.12) | data formatting | bytes 1572864
  110.5 0.0 copy-done
  110.5 0.0 copy-start.1
  110.5 0.8 copy.16
  111.3 0.0 copy-done.1
  111.3 0.5 copy.17
Async XLA Ops:
  108.4 2.1 %copy-start = (f32[27,32,128]{2,1,0:T(8,128)S(1)}, f32[27,32,128]{2,1,0:T(8,128)}, u32[]{:S(2)}) copy-start(f32[27,32,128]{2,1,0:T(8,128)} %get-tuple-element.10) | copy-start | bytes 1327108
  110.5 0.8 copy-start.1

commit v4 on v3

--- a/solution.py
+++ b/solution.py
@@ -30,7 +30,7 @@
     x_ref, w_ref, cot_ref, bias_ref, gat_ref, sca_ref,
     samp_out, dx_out, dw_out, db_out,
     xv, xp, land, halo, wg, cotl, biasb, biasl, im_e, im_o, pacc, part, rsl, rss, sbuf, sland, gbuf, bz, bs, bl,
-    dtmp, dxb, dxp, dxs, dxl, dxo, dwb, dws, dwr, dwl, dwo, dwx, dwy, dwm, dwn, kout, dbo,
+    dtmp, dxb, dxp, dxs, dwb, dws, dwr, dwl, dwo, dwx, dwy, dwm, dwn, kout, dbo,
     v_sem, x_send, x_recv, f_send, h_sem, w_send, w_recv, c_send, c_recv, b_send, b_recv, rs_send, rs_recv,
     s_send, s_recv, ag_send, ag_recv, bz_send, bz_recv, gh_send, gh_recv, bs_send, bs_recv, dxp_send, dxp_recv,
     dx_send, dx_recv, k1_send, k1_recv, k2_send, k2_recv, k3_send, k3_recv, o_sem,
@@ -392,12 +392,12 @@
 
         @pl.when(k == me_k)
         def _():
-            pltpu.make_async_copy(dxs.at[k], dxl.at[z], dx_recv.at[z]).start()
+            pltpu.make_async_copy(dxs.at[k], dx_out.at[z], dx_recv.at[z]).start()
 
         @pl.when(k != me_k)
         def _():
             remote(
-                dxs.at[k], dxl.at[z], dx_send.at[k], dx_recv.at[z], dev(xl, y, xh, lax.div(k, 2), lax.rem(k, 2))
+                dxs.at[k], dx_out.at[z], dx_send.at[k], dx_recv.at[z], dev(xl, y, xh, lax.div(k, 2), lax.rem(k, 2))
             ).start()
 
     def finish_pair(first, second):
@@ -534,6 +534,7 @@
     finish_pair(z_at(3), z_at(4))
     to_x(1)
     to_y(2)
+    y_to_x(0)
     x_to_y(1)
 
     total = bz[z]
@@ -564,7 +565,6 @@
     outs.append(pltpu.make_async_copy(sland, samp_out, o_sem.at[0]))
     outs[-1].start()
 
-    y_to_x(0)
     y_to_x(2)
     for i in range(4):
         landed(dwl.at[1, i, 0], k2_recv.at[4 + i])
@@ -598,14 +598,8 @@
     outs.append(pltpu.make_async_copy(dbo, db_out, o_sem.at[2]))
     outs[-1].start()
 
-    for m in range(4):
-        for i in (2 * m, 2 * m + 1):
-            landed(dxl.at[i], dx_recv.at[i])
-        a, b = dxl[2 * m], dxl[2 * m + 1]
-        dxo[:, m * 128:(m + 1) * 128] = jnp.concatenate([a[:, :64], b[:, :64]], axis=1)
-        dxo[:, 512 + m * 128:512 + (m + 1) * 128] = jnp.concatenate([a[:, 64:], b[:, 64:]], axis=1)
-    outs.append(pltpu.make_async_copy(dxo, dx_out, o_sem.at[3]))
-    outs[-1].start()
+    for i in range(8):
+        landed(dx_out.at[i], dx_recv.at[i])
 
     for end in ends:
         end()
@@ -628,7 +622,7 @@
             @pl.when(k != me_k)
             def _():
                 remote(
-                    dxs.at[k], dxl.at[z], dx_send.at[k], dx_recv.at[z],
+                    dxs.at[k], dx_out.at[z], dx_send.at[k], dx_recv.at[z],
                     dev(xl, y, xh, lax.div(k, 2), lax.rem(k, 2)),
                 ).wait_send()
 
@@ -643,6 +637,30 @@
 
     for out in outs:
         out.wait()
+
+
+def finisher(samp_in, dx_in, dw_in, db_in, samp_out, dx_out, dw_out, db_out, held, made, in_sem, out_sem):
+    loads = [pltpu.make_async_copy(dx_in.at[i], held.at[i], in_sem.at[i]) for i in range(8)]
+    for copy in loads:
+        copy.start()
+    samp_out[...] = samp_in[...]
+    dw_out[...] = dw_in[...]
+    db_out[...] = db_in[...]
+    stores = []
+    for m in range(4):
+        loads[2 * m].wait()
+        loads[2 * m + 1].wait()
+        a, b = held[2 * m], held[2 * m + 1]
+        for half in range(2):
+            cols = pl.ds(half * 512 + m * 128, 128)
+            made[:, cols] = jnp.concatenate(
+                [a[:, half * 64:half * 64 + 64], b[:, half * 64:half * 64 + 64]], axis=1
+            )
+            copy = pltpu.make_async_copy(made.at[:, cols], dx_out.at[:, cols], out_sem.at[2 * m + half])
+            copy.start()
+            stores.append(copy)
+    for copy in stores:
+        copy.wait()
 
 
 def shards(video_clips, weights, conv_bias, cotangent):
@@ -666,7 +684,7 @@
         kernel,
         out_shape=[
             jax.ShapeDtypeStruct((8, 48, 128), BF16),
-            jax.ShapeDtypeStruct((384, 1024), BF16),
+            jax.ShapeDtypeStruct((8, 384, 128), BF16),
             jax.ShapeDtypeStruct((27, 32, 128), F32),
             jax.ShapeDtypeStruct((1, 128), F32),
         ],
@@ -697,8 +715,6 @@
             v((16, 384, 128)),
             v((16, 384, 128)),
             v((16, 384, 128)),
-            v((8, 384, 128)),
-            v((384, 1024)),
             v((3, 2, 2, 9, 32, 512)),
             v((3, 2, 9, 32, 512)),
             v((3, 2, 9, 32, 512)),
@@ -721,6 +737,19 @@
         ),
         cost_estimate=pl.CostEstimate(flops=10_000_000_000, bytes_accessed=8_000_000, transcendentals=50_000),
     )(x, w, cot, bias, gat, sca)
+    samp, dx, dw, db = pl.pallas_call(
+        finisher,
+        out_shape=[
+            jax.ShapeDtypeStruct((8, 48, 128), BF16),
+            jax.ShapeDtypeStruct((384, 1024), BF16),
+            jax.ShapeDtypeStruct((27, 32, 128), F32),
+            jax.ShapeDtypeStruct((1, 128), F32),
+        ],
+        in_specs=[vmem_spec, any_spec, vmem_spec, vmem_spec],
+        out_specs=[vmem_spec, any_spec, vmem_spec, vmem_spec],
+        scratch_shapes=[v((8, 384, 128)), v((384, 1024)), sems(8), sems(8)],
+        cost_estimate=pl.CostEstimate(flops=0, bytes_accessed=3_000_000, transcendentals=0),
+    )(samp, dx, dw, db)
     sampled = samp.reshape(8, 2, 12, 2, 128).transpose(0, 1, 3, 2, 4)
     clip_grad = dx.reshape(1, 4, 4, 24, 1024)
     return sampled, clip_grad, dw.reshape(3, 3, 3, 32, 128), db.reshape(128)

time: 113 us -> 112 us (level)
  local copies, waits for them, and re-layouts: 5.02 us -> 0 us
  Pallas kernels: 106 us -> 109 us
    unnamed x8 -> x0, local copies, waits for them, and re-layouts: 5.02 us -> none
    pallas_call x0 -> x1, Pallas kernels: none -> 4.06 us  [shards(): pl.pallas_call(finisher, out_shape=[jax.ShapeDtypeStruct((8, 48, 128), BF...]
where the time goes in v4:
time: 112 us; the launch traced here: 110 us
  Pallas kernels  109 us (97%)
    pallas_call x1, Pallas kernels, shards(): pl.pallas_call(kernel, out_shape=[jax.ShapeDtypeStruct((8, 48, 128), BF16...  105 us
    pallas_call x1, Pallas kernels, shards(): pl.pallas_call(finisher, out_shape=[jax.ShapeDtypeStruct((8, 48, 128), BF...  4.06 us

profile of v4, /device:TPU:97, one launch (start us, length us, event | category | flops | bytes accessed | tf_op | source)
XLA Modules:
  0.0 110.0 jit_solution(2335810909430615691)
XLA Ops:
  0.6 105.4 %shard_map.93 = (bf16[8,48,128]{2,1,0:T(8,128)(2,1)}, bf16[8,384,128]{2,1,0:T(8,128)(2,1)}, f32[27,32,128]{2,1,0:T(8,128)}, f32[1,128]{1,0:T(1,128)}) custom-call(bf16[384,1024]{1,0:T(8,128)(2,1)} %bitcast.12, bf16[27,32,128]{2,1,0:T(8,128)(2,1)} %bitcast.15, bf16[8,48,128]{2,1,0:T(8,128)(2,1)} %bitcast.16, f32[1,128]{1,0:T(1,128)} %bitcast.18, ...), custom_call_target="tpu_custom_call" | custom-call | flops 10000000000 | bytes 8000000 | tf_op jit(solution)/shard_map/pallas_call | solution.py:683
  106.0 4.1 %shard_map.94 = (bf16[8,48,128]{2,1,0:T(8,128)(2,1)}, bf16[384,1024]{1,0:T(8,128)(2,1)}, f32[27,32,128]{2,1,0:T(8,128)}, f32[1,128]{1,0:T(1,128)}) custom-call(bf16[8,48,128]{2,1,0:T(8,128)(2,1)} %get-tuple-element.12.samp_in, bf16[8,384,128]{2,1,0:T(8,128)(2,1)} %get-tuple-element.13.dx_in, f32[27,32,128]{2,1,0:T(8,128)} %get-tuple-element.14.dw_in, ...), custom_call_target="tpu_custom_call" | custom-call | bytes 3000000 | tf_op jit(solution)/shard_map/pallas_call | solution.py:740

commit v5 on v4

--- a/solution.py
+++ b/solution.py
@@ -88,7 +88,7 @@
     ends = []
 
     me_k = 2 * z + c
-    for n, dz in enumerate((4, 3, 5, 2, 6, 1, 7)):
+    for n, dz in enumerate((1, 7, 4, 3, 5, 2, 6)):
         zt = plus(z, dz, 8)
         copy = remote(xp.at[zt], land.at[me_k], x_send.at[n], x_recv.at[me_k], dev(xl, y, xh, zt, xl))
         copy.start()
@@ -146,8 +146,15 @@
     ends.append(halo_copy.wait_send)
 
     def place_of(j):
-        far = jnp.where(lax.rem(j, 2) == 0, 4 - lax.div(j, 2), 4 + lax.div(j, 2))
-        return plus(z, jnp.where(j == 0, 0, far), 8)
+        dz = 0
+        dz = jnp.where(j == 1, 1, dz)
+        dz = jnp.where(j == 2, 7, dz)
+        dz = jnp.where(j == 3, 4, dz)
+        dz = jnp.where(j == 4, 3, dz)
+        dz = jnp.where(j == 5, 5, dz)
+        dz = jnp.where(j == 6, 2, dz)
+        dz = jnp.where(j == 7, 6, dz)
+        return plus(z, dz, 8)
 
     def pass_on(first, last):
         @pl.when(primary)
@@ -270,8 +277,8 @@
 
     forward((4, -3))
     rs_step(1)
+    take_in(6, 8)
     forward((3, -2))
-    take_in(6, 8)
     rs_step(2)
     forward((2, -1, 1))
     rs_step(3)
@@ -332,23 +339,25 @@
 
     sums = jnp.sum(slope, axis=0, keepdims=True)
     bz[z] = jnp.concatenate([sums[:, i * 128:(i + 1) * 128] for i in range(4)] + [jnp.zeros((4, 128), F32)], axis=0)
-    for n, dz in enumerate((1, 7, 2, 6, 3, 5, 4)):
-        copy = remote(bz.at[z], bz.at[z], bz_send.at[n], bz_recv.at[z], dev(xl, y, xh, plus(z, dz, 8), c))
-        copy.start()
-        ends.append(copy.wait_send)
     for cs in range(2):
         for i in range(4):
             sbuf[cs, i] = samp[cs * 48:(cs + 1) * 48, i * 128:(i + 1) * 128]
-    for dy in range(4):
-        for dc in range(2):
-            yd, cd = plus(y, dy, 4), plus(c, dc, 2)
-            src, dst, sem = sbuf.at[cd, yd], sland.at[c * 4 + y], s_recv.at[c * 4 + y]
-            if dy or dc:
-                copy = remote(src, dst, s_send.at[dy * 2 + dc], sem, dev(xl, yd, xh, z, cd))
-                copy.start()
-                ends.append(copy.wait_send)
-            else:
-                pltpu.make_async_copy(src, dst, sem).start()
+
+    def late_sends():
+        for n, dz in enumerate((1, 7, 2, 6, 3, 5, 4)):
+            copy = remote(bz.at[z], bz.at[z], bz_send.at[n], bz_recv.at[z], dev(xl, y, xh, plus(z, dz, 8), c))
+            copy.start()
+            ends.append(copy.wait_send)
+        for dy in range(4):
+            for dc in range(2):
+                yd, cd = plus(y, dy, 4), plus(c, dc, 2)
+                src, dst, sem = sbuf.at[cd, yd], sland.at[c * 4 + y], s_recv.at[c * 4 + y]
+                if dy or dc:
+                    copy = remote(src, dst, s_send.at[dy * 2 + dc], sem, dev(xl, yd, xh, z, cd))
+                    copy.start()
+                    ends.append(copy.wait_send)
+                else:
+                    pltpu.make_async_copy(src, dst, sem).start()
 
     def back_pair(first, second):
         def back(h, carry):
@@ -425,6 +434,8 @@
                 landed(gbuf.at[8, pl.ds(0, 32)], gh_recv.at[0])
 
         back_pair(z_at(step - 1), z_at(-step))
+        if step == 1:
+            late_sends()
         if step > 1:
             finish_pair(z_at(step - 2), z_at(1 - step))
     for half in range(2):

time: 112 us -> 109 us (0.973); the launches traced: 110 us -> 108 us
    pallas_call x1, Pallas kernels: 105 us -> 104 us  [shards(): pl.pallas_call(kernel, out_shape=[jax.ShapeDtypeStruct((8, 48, 128), BF16...]
where the time goes in v5:
time: 109 us; the launch traced here: 108 us
  Pallas kernels  108 us (99%)
    pallas_call x1, Pallas kernels, shards(): pl.pallas_call(kernel, out_shape=[jax.ShapeDtypeStruct((8, 48, 128), BF16...  104 us
    pallas_call x1, Pallas kernels, shards(): pl.pallas_call(finisher, out_shape=[jax.ShapeDtypeStruct((8, 48, 128), BF...  4.06 us

profile of v5, /device:TPU:97, one launch (start us, length us, event | category | flops | bytes accessed | tf_op | source)
XLA Modules:
  0.0 108.4 jit_solution(799392920655446055)
XLA Ops:
  0.6 103.7 %shard_map.93 = (bf16[8,48,128]{2,1,0:T(8,128)(2,1)}, bf16[8,384,128]{2,1,0:T(8,128)(2,1)}, f32[27,32,128]{2,1,0:T(8,128)}, f32[1,128]{1,0:T(1,128)}) custom-call(bf16[384,1024]{1,0:T(8,128)(2,1)} %bitcast.12, bf16[27,32,128]{2,1,0:T(8,128)(2,1)} %bitcast.15, bf16[8,48,128]{2,1,0:T(8,128)(2,1)} %bitcast.16, f32[1,128]{1,0:T(1,128)} %bitcast.18, ...), custom_call_target="tpu_custom_call" | custom-call | flops 10000000000 | bytes 8000000 | tf_op jit(solution)/shard_map/pallas_call | solution.py:694
  104.4 4.1 %shard_map.94 = (bf16[8,48,128]{2,1,0:T(8,128)(2,1)}, bf16[384,1024]{1,0:T(8,128)(2,1)}, f32[27,32,128]{2,1,0:T(8,128)}, f32[1,128]{1,0:T(1,128)}) custom-call(bf16[8,48,128]{2,1,0:T(8,128)(2,1)} %get-tuple-element.12.samp_in, bf16[8,384,128]{2,1,0:T(8,128)(2,1)} %get-tuple-element.13.dx_in, f32[27,32,128]{2,1,0:T(8,128)} %get-tuple-element.14.dw_in, ...), custom_call_target="tpu_custom_call" | custom-call | bytes 3000000 | tf_op jit(solution)/shard_map/pallas_call | solution.py:751

commit v6 on v5

--- a/solution.py
+++ b/solution.py
@@ -88,7 +88,7 @@
     ends = []
 
     me_k = 2 * z + c
-    for n, dz in enumerate((1, 7, 4, 3, 5, 2, 6)):
+    for n, dz in enumerate((4, 1, 7, 3, 5, 2, 6)):
         zt = plus(z, dz, 8)
         copy = remote(xp.at[zt], land.at[me_k], x_send.at[n], x_recv.at[me_k], dev(xl, y, xh, zt, xl))
         copy.start()
@@ -147,9 +147,9 @@
 
     def place_of(j):
         dz = 0
-        dz = jnp.where(j == 1, 1, dz)
-        dz = jnp.where(j == 2, 7, dz)
-        dz = jnp.where(j == 3, 4, dz)
+        dz = jnp.where(j == 1, 4, dz)
+        dz = jnp.where(j == 2, 1, dz)
+        dz = jnp.where(j == 3, 7, dz)
         dz = jnp.where(j == 4, 3, dz)
         dz = jnp.where(j == 5, 5, dz)
         dz = jnp.where(j == 6, 2, dz)

time: 109 us -> 108 us (level)
  no operation moved by 1% of the time
where the time goes in v6:
time: 108 us; the launch traced here: 107 us
  Pallas kernels  107 us (99%)
    pallas_call x1, Pallas kernels, shards(): pl.pallas_call(kernel, out_shape=[jax.ShapeDtypeStruct((8, 48, 128), BF16...  103 us
    pallas_call x1, Pallas kernels, shards(): pl.pallas_call(finisher, out_shape=[jax.ShapeDtypeStruct((8, 48, 128), BF...  4.06 us

profile of v6, /device:TPU:97, one launch (start us, length us, event | category | flops | bytes accessed | tf_op | source)
XLA Modules:
  0.0 107.5 jit_solution(1068182964017078191)
XLA Ops:
  0.6 102.8 %shard_map.93 = (bf16[8,48,128]{2,1,0:T(8,128)(2,1)}, bf16[8,384,128]{2,1,0:T(8,128)(2,1)}, f32[27,32,128]{2,1,0:T(8,128)}, f32[1,128]{1,0:T(1,128)}) custom-call(bf16[384,1024]{1,0:T(8,128)(2,1)} %bitcast.12, bf16[27,32,128]{2,1,0:T(8,128)(2,1)} %bitcast.15, bf16[8,48,128]{2,1,0:T(8,128)(2,1)} %bitcast.16, f32[1,128]{1,0:T(1,128)} %bitcast.18, ...), custom_call_target="tpu_custom_call" | custom-call | flops 10000000000 | bytes 8000000 | tf_op jit(solution)/shard_map/pallas_call | solution.py:694
  103.4 4.1 %shard_map.94 = (bf16[8,48,128]{2,1,0:T(8,128)(2,1)}, bf16[384,1024]{1,0:T(8,128)(2,1)}, f32[27,32,128]{2,1,0:T(8,128)}, f32[1,128]{1,0:T(1,128)}) custom-call(bf16[8,48,128]{2,1,0:T(8,128)(2,1)} %get-tuple-element.12.samp_in, bf16[8,384,128]{2,1,0:T(8,128)(2,1)} %get-tuple-element.13.dx_in, f32[27,32,128]{2,1,0:T(8,128)} %get-tuple-element.14.dw_in, ...), custom_call_target="tpu_custom_call" | custom-call | bytes 3000000 | tf_op jit(solution)/shard_map/pallas_call | solution.py:751

commit v7 on v6

--- a/solution.py
+++ b/solution.py
@@ -87,23 +87,6 @@
 
     ends = []
 
-    me_k = 2 * z + c
-    for n, dz in enumerate((4, 1, 7, 3, 5, 2, 6)):
-        zt = plus(z, dz, 8)
-        copy = remote(xp.at[zt], land.at[me_k], x_send.at[n], x_recv.at[me_k], dev(xl, y, xh, zt, xl))
-        copy.start()
-        ends.append(copy.wait_send)
-    own_x = pltpu.make_async_copy(xp.at[z], land.at[me_k], x_recv.at[me_k])
-    sib_x = remote(xp.at[z], land.at[me_k], x_send.at[7], x_recv.at[me_k], dev(xl, y, xh, z, 1 - c))
-
-    @pl.when(primary)
-    def _():
-        own_x.start()
-
-    @pl.when(jnp.logical_not(primary))
-    def _():
-        sib_x.start()
-
     def w_at(h_, c_, y_):
         return wg.at[:, pl.ds(pl.multiple_of((h_ * 2 + c_) * 32, 32), 32), pl.ds(pl.multiple_of(y_ * 128, 128), 128)]
 
@@ -125,6 +108,23 @@
     w_push(w_ref, xh, c, y, dev_down)
     w_push(w_ref, xh, c, y, sibling)
     pltpu.make_async_copy(w_ref, w_at(xh, c, y), w_sem(xh, c, y)).start()
+
+    me_k = 2 * z + c
+    for n, dz in enumerate((4, 1, 7, 3, 5, 2, 6)):
+        zt = plus(z, dz, 8)
+        copy = remote(xp.at[zt], land.at[me_k], x_send.at[n], x_recv.at[me_k], dev(xl, y, xh, zt, xl))
+        copy.start()
+        ends.append(copy.wait_send)
+    own_x = pltpu.make_async_copy(xp.at[z], land.at[me_k], x_recv.at[me_k])
+    sib_x = remote(xp.at[z], land.at[me_k], x_send.at[7], x_recv.at[me_k], dev(xl, y, xh, z, 1 - c))
+
+    @pl.when(primary)
+    def _():
+        own_x.start()
+
+    @pl.when(jnp.logical_not(primary))
+    def _():
+        sib_x.start()
 
     for dy in range(4):
         for dc in range(2):

time: 108 us -> 108 us (level)
  no operation moved by 1% of the time
where the time goes in v7:
time: 108 us
  Pallas kernels  107 us (99%)
    pallas_call x1, Pallas kernels, shards(): pl.pallas_call(kernel, out_shape=[jax.ShapeDtypeStruct((8, 48, 128), BF16...  103 us
    pallas_call x1, Pallas kernels, shards(): pl.pallas_call(finisher, out_shape=[jax.ShapeDtypeStruct((8, 48, 128), BF...  4.06 us

profile of v7, /device:TPU:97, one launch (start us, length us, event | category | flops | bytes accessed | tf_op | source)
XLA Modules:
  0.0 107.5 jit_solution(9867221351858920939)
XLA Ops:
  0.6 102.8 %shard_map.93 = (bf16[8,48,128]{2,1,0:T(8,128)(2,1)}, bf16[8,384,128]{2,1,0:T(8,128)(2,1)}, f32[27,32,128]{2,1,0:T(8,128)}, f32[1,128]{1,0:T(1,128)}) custom-call(bf16[384,1024]{1,0:T(8,128)(2,1)} %bitcast.12, bf16[27,32,128]{2,1,0:T(8,128)(2,1)} %bitcast.15, bf16[8,48,128]{2,1,0:T(8,128)(2,1)} %bitcast.16, f32[1,128]{1,0:T(1,128)} %bitcast.18, ...), custom_call_target="tpu_custom_call" | custom-call | flops 10000000000 | bytes 8000000 | tf_op jit(solution)/shard_map/pallas_call | solution.py:694
  103.5 4.1 %shard_map.94 = (bf16[8,48,128]{2,1,0:T(8,128)(2,1)}, bf16[384,1024]{1,0:T(8,128)(2,1)}, f32[27,32,128]{2,1,0:T(8,128)}, f32[1,128]{1,0:T(1,128)}) custom-call(bf16[8,48,128]{2,1,0:T(8,128)(2,1)} %get-tuple-element.12.samp_in, bf16[8,384,128]{2,1,0:T(8,128)(2,1)} %get-tuple-element.13.dx_in, f32[27,32,128]{2,1,0:T(8,128)} %get-tuple-element.14.dw_in, ...), custom_call_target="tpu_custom_call" | custom-call | bytes 3000000 | tf_op jit(solution)/shard_map/pallas_call | solution.py:751
